TPU v7x, 32 devices: a whole 2x2x4 slice. The times are simulated.
32 devices in a mesh: row: 4 (over y, x), col: 2 (over core), layer: 4 (over z).
Axes of the slice: x: 2, y: 2, z: 4, core: 2. Of those that a mesh axis runs over, the one named last changes fastest.
Arguments:
- density: bfloat16 [8192, 8192], P('row', 'col'), may hold values from -0.59765625 to 0.59765625
- density_pattern: int32 [64, 64], replicated, may hold values from 0 to 1, as said below
- result_pattern: int32 [64, 64], replicated, may hold values from 0 to 1, as said below
Outputs:
- purified: bfloat16 [8192, 4, 2048], P('row', 'layer', 'col')
Inputs may be any that keep to these rules, and one draw needn't show every extreme that they name: `density_pattern`: symmetric, with ones on the diagonal; blocks are atom clusters in a periodic chain, and a block row keeps the blocks within a cutoff distance of its cluster that varies from row to row. `result_pattern`: symmetric; keeps the blocks within a somewhat larger cutoff distance than density_pattern.
All inputs are finite; a program needn't handle non-finite values.
Results may differ from a plain program's by a relative error of at most 0.017.
Values may be sent and summed in bfloat16 or wider, within the bound.
No kernel may reach another device: no remote copies, remote signals or barrier semaphores. Data moves between devices by JAX's collectives and lax.ppermute only.
A program may use at most 128 MiB of HBM per device.

v0:
```python
import jax
import jax.numpy as jnp
from jax import lax
from jax.sharding import PartitionSpec as P

B = 128


def shards(density, density_pattern, result_pattern):
    rows_here, cols_here = density.shape
    layers = lax.axis_size("layer")
    block_rows = rows_here // B
    block_cols = cols_here // B
    row_index = lax.axis_index("row")
    col_index = lax.axis_index("col")
    layer_index = lax.axis_index("layer")
    mask_here = lax.dynamic_slice(
        density_pattern, (row_index * block_rows, col_index * block_cols), (block_rows, block_cols)
    )
    tile_here = (
        density.reshape(block_rows, B, block_cols, B)
        * mask_here.astype(jnp.bfloat16)[:, None, :, None]
    )
    regrouped = (
        tile_here.reshape(block_rows, B, block_cols // layers, layers, B)
        .transpose(0, 1, 3, 2, 4)
        .reshape(rows_here, cols_here)
    )
    group_width = cols_here // layers
    own_columns = lax.dynamic_slice_in_dim(regrouped, layer_index * group_width, group_width, 1)
    own_rows = lax.dynamic_index_in_dim(
        regrouped.reshape(block_rows // layers, layers, B, cols_here),
        layer_index,
        1,
        keepdims=False,
    )
    own_rows = own_rows.reshape(rows_here // layers, cols_here)
    col_panel = lax.all_gather(own_rows, "row", axis=0, tiled=True)

    def add_product(segment):
        return jnp.dot(segment, col_panel, preferred_element_type=jnp.float32)

    partial_square = add_product(lax.all_gather(own_columns, "col", axis=1, tiled=True))
    square = lax.psum_scatter(
        partial_square.astype(jnp.bfloat16), "layer", scatter_dimension=1, tiled=True
    ).astype(jnp.float32)
    square_rounded = square.astype(jnp.bfloat16)
    partial_cube = add_product(lax.all_gather(square_rounded, "col", axis=1, tiled=True))
    cube = lax.psum_scatter(
        partial_cube.astype(jnp.bfloat16), "layer", scatter_dimension=1, tiled=True
    ).astype(jnp.float32)
    keep_here = lax.dynamic_slice(
        result_pattern, (row_index * block_rows, col_index * block_cols), (block_rows, block_cols)
    )
    keep_group = lax.dynamic_index_in_dim(
        keep_here.reshape(block_rows, block_cols // layers, layers), layer_index, 2, keepdims=False
    )
    combined = (3.0 * square - 2.0 * cube).reshape(block_rows, B, block_cols // layers, B)
    combined = combined * keep_group.astype(jnp.float32)[:, None, :, None]
    return combined.reshape(rows_here, 1, group_width).astype(jnp.bfloat16)


def solution(mesh):
    return jax.shard_map(
        shards,
        mesh=mesh,
        in_specs=(P("row", "col"), P(), P()),
        out_specs=P("row", "layer", "col"),
        check_vma=False,
    )
```

profile of v0, /device:TPU:0, one launch (start us, length us, event | category | flops | bytes accessed | tf_op | source)
XLA Modules:
  0.0 1007.6 jit_solution(9588810583647798553)
XLA Ops:
  6.5 0.8 dynamic_slice.17
  7.3 0.1 copy.18
  7.4 27.3 %reshape.33 = bf16[16,128,8,4,128]{4,3,2,1,0:T(4,128)(2,1)} reshape(bf16[2048,4096]{1,0:T(8,128)(2,1)} %param.3) | data formatting | bytes 33554432 | tf_op jit(solution)/shard_map/reshape | solution.py:21
  34.7 20.8 %copy.17 = bf16[16,128,8,4,128]{1,0,4,3,2:T(8,128)(2,1)} copy(bf16[16,128,8,4,128]{4,3,2,1,0:T(4,128)(2,1)} %reshape.33) | data formatting | bytes 33554432 | tf_op jit(solution)/shard_map/reshape | solution.py:21
  55.5 13.9 %multiply_bitcast_fusion = bf16[16,128,4,8,128]{1,0,4,2,3:T(8,128)(2,1)} fusion(bf16[16,128,8,4,128]{1,0,4,3,2:T(8,128)(2,1)} %copy.17, bf16[16,8,4]{0,2,1:T(4,128)(2,1)S(1)} %bitcast.26), kind=kLoop, calls=%fused_computation | loop fusion | flops 8388608 | bytes 33555456 | tf_op jit(solution)/shard_map/transpose | solution.py:26
  69.4 37.2 %copy.12 = bf16[16,128,4,8,128]{4,3,2,1,0:T(8,128)(2,1)} copy(bf16[16,128,4,8,128]{1,0,4,2,3:T(8,128)(2,1)} %multiply_bitcast_fusion) | data formatting | bytes 33554432 | tf_op jit(solution)/shard_map/transpose | solution.py:26
  106.6 25.3 %reshape.30 = bf16[2048,4096]{1,0:T(8,128)(2,1)} reshape(bf16[16,128,4,8,128]{4,3,2,1,0:T(8,128)(2,1)} %copy.12) | data formatting | bytes 33554432 | tf_op jit(solution)/shard_map/reshape | solution.py:27
  131.9 4.6 constant_dynamic-slice_fusion.1
  136.6 15.8 %copy.13 = bf16[16,128,4,8,128]{1,4,3,2,0:T(8,128)(2,1)} copy(bf16[16,128,4,8,128]{1,0,4,2,3:T(8,128)(2,1)} %multiply_bitcast_fusion) | data formatting | bytes 33554432 | tf_op jit(solution)/shard_map/transpose | solution.py:26
  152.4 5.3 constant_dynamic-slice_fusion
  157.7 6.4 copy.14
  164.2 160.1 %all-gather.6.cloned.1.call-done = bf16[2048,4096]{1,0:T(8,128)(2,1)} async-done(((bf16[512,4096]{1,0:T(8,128)(2,1)}), bf16[2048,4096]{1,0:T(8,128)(2,1)}) %all-gather.6.cloned.1.call-update) | async-done | bytes 16777232 | tf_op jit(solution)/shard_map/all_gather | solution.py:38
  324.3 41.8 %convolution_convert_fusion.1 = bf16[2048,4096]{1,0:T(8,128)(2,1)} fusion(bf16[2048,2048]{1,0:T(8,128)(2,1)} %all-gather.4.cloned.1.call-done, bf16[2048,4096]{1,0:T(8,128)(2,1)} %all-gather.6.cloned.1.call-done), kind=kOutput, calls=%fused_computation.2 | convolution fusion | flops 34368126976 | bytes 41943040 | tf_op jit(solution)/shard_map/dot_general | solution.py:41
  366.2 280.4 %reduce-scatter.3.cloned.1.call-done = bf16[2048,1024]{1,0:T(8,128)(2,1)} async-done(((bf16[2048,4096]{1,0:T(8,128)(2,1)}), bf16[2048,1024]{1,0:T(8,128)(2,1)}) %reduce-scatter.3.cloned.1.call-update) | async-done | bytes 4194320 | tf_op jit(solution)/shard_map/reduce_scatter | solution.py:44
  646.6 0.2 reduce-scatter.5.cloned.1.call-start
  646.8 21.8 %all-gather.8.cloned.1.call-done = bf16[2048,2048]{1,0:T(8,128)(2,1)} async-done(((bf16[2048,1024]{1,0:T(8,128)(2,1)}), bf16[2048,2048]{1,0:T(8,128)(2,1)}) %all-gather.8.cloned.1.call-update) | async-done | bytes 8388624 | tf_op jit(solution)/shard_map/all_gather | solution.py:48
  668.6 41.8 %convolution_convert_fusion = bf16[2048,4096]{1,0:T(8,128)(2,1)} fusion(bf16[2048,2048]{1,0:T(8,128)(2,1)} %all-gather.8.cloned.1.call-done, bf16[2048,4096]{1,0:T(8,128)(2,1)} %all-gather.6.cloned.1.call-done), kind=kOutput, calls=%fused_computation.1 | convolution fusion | flops 34368126976 | bytes 41943040 | tf_op jit(solution)/shard_map/dot_general | solution.py:41
  710.4 0.8 dynamic_slice.20
  711.2 0.1 copy.19
  711.4 280.7 %reduce-scatter.5.cloned.1.call-done = bf16[2048,1024]{1,0:T(8,128)(2,1)} async-done(((bf16[2048,4096]{1,0:T(8,128)(2,1)}), bf16[2048,1024]{1,0:T(8,128)(2,1)}) %reduce-scatter.5.cloned.1.call-update) | async-done | bytes 4194320 | tf_op jit(solution)/shard_map/reduce_scatter | solution.py:49
  992.1 0.6 mul.55
  992.7 1.6 copy-done
  994.3 1.3 copy-done.1
  995.6 5.5 fusion.1
  (15 shorter events, 0.3 us)
Async XLA Ops:
  6.5 157.7 %all-gather.4.cloned.1.call-start = ((), (), s32[]{:S(2)}) async-start(), calls=%async_computation.2 | async-start | bytes 12582912 | tf_op jit(solution)/shard_map/all_gather | solution.py:43
  136.6 187.7 %all-gather.6.cloned.1.call-start = ((), (), s32[]{:S(2)}) async-start(), calls=%async_computation.3 | async-start | bytes 20971520 | tf_op jit(solution)/shard_map/all_gather | solution.py:38
  164.1 482.4 %reduce-scatter.3.cloned.1.call-start = ((), (), s32[]{:S(2)}) async-start(), calls=%async_computation.4 | async-start | bytes 20971520 | tf_op jit(solution)/shard_map/reduce_scatter | solution.py:44
  366.1 302.5 %all-gather.8.cloned.1.call-start = ((), (), s32[]{:S(2)}) async-start(), calls=%async_computation.5 | async-start | bytes 12582912 | tf_op jit(solution)/shard_map/all_gather | solution.py:48
  646.6 345.5 %reduce-scatter.5.cloned.1.call-start = ((), (), s32[]{:S(2)}) async-start(), calls=%async_computation.6 | async-start | bytes 20971520 | tf_op jit(solution)/shard_map/reduce_scatter | solution.py:49
  992.1 2.2 copy-start
  992.1 3.5 copy-start.1
Sparse Core Ops, SparseCore 0:
  136.7 22.5 all-gather.3
  164.3 160.0 all-gather.5
  366.2 280.2 reduce-scatter.2
  648.0 20.5 all-gather.7
  710.6 281.4 reduce-scatter.4
where the time goes:
time: 1010 us
  waiting for transfers between devices  743 us (74%)
  local copies, waits for them, and re-layouts  148 us (15%)
  matrix products  83.5 us (8%)
  other arithmetic  19.4 us (2%)
  between operations  13.2 us (1%)
    reduce_scatter x1, waiting for transfers between devices, shards(): lax.psum_scatter(partial_cube.astype(jnp.bfloat16), 'layer', scatter_dime...  281 us
    reduce_scatter x1, waiting for transfers between devices, shards(): lax.psum_scatter(partial_square.astype(jnp.bfloat16), 'layer', scatter_di...  280 us
    all_gather x1, waiting for transfers between devices, shards(): col_panel = lax.all_gather(own_rows, 'row', axis=0, tiled=True)  160 us
    dot_general x2, matrix products, add_product(): return jnp.dot(segment, col_panel, preferred_element_type=jnp.float32)  83.5 us
    transpose x2, local copies, waits for them, and re-layouts, shards(): regrouped = tile_here.reshape(block_rows, B, block_cols // layers, layers...  53 us
    reshape x2, local copies, waits for them, and re-layouts, shards(): density.reshape(block_rows, B, block_cols, B)  48.1 us
    reshape x1, local copies, waits for them, and re-layouts, shards(): regrouped = tile_here.reshape(block_rows, B, block_cols // layers, layers...  25.3 us
    all_gather x1, waiting for transfers between devices, shards(): lax.all_gather(square_rounded, 'col', axis=1, tiled=True)  21.8 us
  transfers between devices with their start and end apart: 5, of which 4 were waited for; matrix products, arithmetic and copies ran while one was open for 3% of the time, Pallas kernels for 0%

commit v1 on v0

v1 whole, which is shorter than its diff:
```python
import functools

import jax
import jax.numpy as jnp
from jax import lax
from jax.experimental import pallas as pl
from jax.experimental.pallas import tpu as pltpu
from jax.sharding import PartitionSpec as P

B = 128
STEP = 4
TILE = 2
VMEM = 56 * 2**20


def swap(x, axis, distance):
    size = lax.axis_size(axis)
    return lax.ppermute(x, axis, [(i, i ^ distance) for i in range(size)])


def after(x, *earlier):
    return lax.optimization_barrier((x, *earlier))[0]


def exchange(own, gate):
    half = own.shape[0] // 2
    if gate is not None:
        own = after(own, *gate)
    across = swap(own, "row", 1)
    along = swap(own, "row", 2)
    far_top = swap(across[:half], "row", 2)
    far_bottom = swap(along[half:], "row", 1)
    return across, along, far_top, far_bottom


def pick_kernel(start, where, keep, x_ref, o_ref):
    q = pl.program_id(0)
    for i in range(x_ref.shape[0] // B):
        rows = pl.ds(i * B, B)
        kept = keep[i, start + q] != 0
        o_ref[rows, :] = jnp.where(kept, x_ref[rows, :], jnp.zeros((B, B), o_ref.dtype))


def pick_columns(density, keep, layer, layers, start, group):
    rows = density.shape[0]
    return pl.pallas_call(
        functools.partial(pick_kernel, start),
        grid_spec=pltpu.PrefetchScalarGridSpec(
            num_scalar_prefetch=2,
            grid=(group,),
            in_specs=[pl.BlockSpec((rows, B), lambda q, where, keep: (0, (start + q) * layers + where[0]))],
            out_specs=pl.BlockSpec((rows, B), lambda q, where, keep: (0, q)),
        ),
        out_shape=jax.ShapeDtypeStruct((rows, group * B), density.dtype),
        compiler_params=pltpu.CompilerParams(vmem_limit_bytes=VMEM),
        name="pick_columns",
    )(jnp.reshape(layer, (1,)), keep, density)


def product_kernel(plan, n_src, splits, first, last, column, meta, active, keep, *refs):
    refs = list(refs)
    take = lambda n: [refs.pop(0) for _ in range(n)]
    n_part = len(plan)
    lhs = [take(n_src) for _ in range(n_part)]
    masks = take(n_part)
    panels = [take(n) for n in splits]
    total_in = None if first else take(1)[0]
    square_in = take(1)[0] if last else None
    if last and column > 0:
        take(1)
    outs = refs[:-1]
    total = refs[-1]
    i = pl.program_id(0)
    tile = total.shape[0]
    total[...] = jnp.zeros_like(total) if first else total_in[...]
    for p, m in enumerate(plan):
        source, owner = meta[3 * m], meta[3 * m + 2]
        depth = lhs[p][0].shape[1]
        steps = depth // (STEP * B)
        piece = depth // splits[p]
        for s in range(steps):
            cols = pl.ds(s * STEP * B, STEP * B)
            at = s * STEP * B
            panel = panels[p][at // piece]
            used = active[i, owner * steps + s] != 0
            for h in range(n_src):
                @pl.when(used & (source == h) if n_src > 1 else used)
                def _():
                    kept = [
                        jnp.broadcast_to(masks[p][0, t:t + 1, cols], (B, STEP * B))
                        for t in range(tile // B)
                    ]
                    kept = jnp.concatenate(kept, axis=0).astype(jnp.bfloat16)
                    total[...] += jnp.dot(
                        lhs[p][h][:, cols] * kept,
                        panel[pl.ds(at % piece, STEP * B), :],
                        preferred_element_type=jnp.float32,
                    )
    if not last:
        outs[0][...] = total[...]
        if len(outs) > 1:
            outs[1][...] = total[...].astype(outs[1].dtype)
        return
    step = total.shape[1] // B
    for t in range(tile // B):
        for q in range(step):
            at = (pl.ds(t * B, B), pl.ds(q * B, B))
            value = 3.0 * square_in[at] - 2.0 * total[at]
            kept = keep[i * (tile // B) + t, column * step + q] != 0
            outs[0][at] = jnp.where(kept, value, 0.0).astype(outs[0].dtype)


def product(plan, meta, active, keep, sources, mask, panels, total=None, rounded=False,
            square=None, out=None, column=0):
    rows = sources[0].shape[0]
    width = panels[0][0].shape[1]
    tile = TILE * B
    n_src = len(sources)
    depth = rows
    first, last = total is None, square is not None
    specs, args = [], []
    for m in plan:
        for h in range(n_src):
            def index(i, meta, active, keep, m=m, h=h):
                here = meta[3 * m] == h
                return jnp.where(here, i, 0), jnp.where(here, meta[3 * m + 1], 0)
            specs.append(pl.BlockSpec((tile, depth), index))
            args.append(sources[h])
    for m in plan:
        specs.append(pl.BlockSpec((1, TILE, depth), lambda i, meta, active, keep, m=m: (i, 0, meta[3 * m + 2])))
        args.append(mask)
    for group in panels:
        for panel in group:
            specs.append(pl.BlockSpec(panel.shape, lambda i, *_: (0, 0), pipeline_mode=pl.Buffered(1)))
            args.append(panel)
    row_block = pl.BlockSpec((tile, width), lambda i, *_: (i, 0))
    if not first:
        specs.append(row_block)
        args.append(total)
    aliases = {}
    if last:
        specs.append(row_block)
        args.append(square)
        if column > 0:
            specs.append(pl.BlockSpec(memory_space=pl.ANY))
            args.append(out)
            aliases = {3 + len(args) - 1: 0}
        out_shape = [jax.ShapeDtypeStruct(out if column == 0 else out.shape, jnp.bfloat16)]
        out_specs = [pl.BlockSpec((tile, width), lambda i, *_: (i, column))]
    else:
        out_shape = [jax.ShapeDtypeStruct((rows, width), jnp.float32)]
        out_specs = [row_block]
        if rounded:
            out_shape.append(jax.ShapeDtypeStruct((rows, width), jnp.bfloat16))
            out_specs.append(row_block)
    flops = 2 * rows * depth * len(plan) * width
    result = pl.pallas_call(
        functools.partial(product_kernel, plan, n_src, [len(g) for g in panels], first, last, column),
        grid_spec=pltpu.PrefetchScalarGridSpec(
            num_scalar_prefetch=3,
            grid=(rows // tile,),
            in_specs=specs,
            out_specs=out_specs,
            scratch_shapes=[pltpu.VMEM((tile, width), jnp.float32)],
        ),
        out_shape=out_shape,
        input_output_aliases=aliases,
        cost_estimate=pl.CostEstimate(
            flops=flops, bytes_accessed=2 * rows * depth * len(plan), transcendentals=0),
        compiler_params=pltpu.CompilerParams(vmem_limit_bytes=VMEM),
        name="product",
    )(meta, active, keep, *args)
    return result if rounded else result[0]


def shards(density, density_pattern, result_pattern):
    rows, cols = density.shape
    layers = lax.axis_size("layer")
    n_col = lax.axis_size("col")
    block_rows, block_cols = rows // B, cols // B
    group = block_cols // layers
    width = group * B
    r, c, l = (lax.axis_index(a) for a in ("row", "col", "layer"))
    n_chunk = 2 if group % 4 == 0 else 1
    chunk_w = width // n_chunk

    def pattern_tile(pattern):
        here = lax.dynamic_slice(pattern, (r * block_rows, c * block_cols), (block_rows, block_cols))
        return lax.dynamic_index_in_dim(here.reshape(block_rows, group, layers), l, 2, keepdims=False)

    if n_col == 2:
        sources = [density, swap(density, "col", 1)]
    else:
        sources = [lax.all_gather(density, "col", axis=1, tiled=True)]
    own_mask = pattern_tile(density_pattern)
    step = group // n_chunk
    own_chunks = [
        pick_columns(density, own_mask, l, layers, j * step, step) for j in range(n_chunk)
    ]
    row_mask = lax.dynamic_slice_in_dim(density_pattern, r * block_rows, block_rows, 0)
    n_block = row_mask.shape[1]
    active = row_mask.reshape(block_rows // TILE, TILE, n_block // STEP, STEP).max(axis=(1, 3))
    mask = jnp.repeat(row_mask.astype(jnp.float32), B, axis=1)
    mask = mask.reshape(block_rows // TILE, TILE, n_block * B)
    keep = pattern_tile(result_pattern)
    meta = []
    per_source = n_block * B // rows // len(sources)
    for m in range(4):
        owner = r ^ m
        source = (owner // per_source != c) if len(sources) == 2 else 0
        meta += [source, owner % per_source, owner]
    meta = jnp.stack([jnp.asarray(v, jnp.int32) for v in meta])
    run = functools.partial(product, meta=meta, active=active, keep=keep, sources=sources, mask=mask)

    gate = None
    density_panels = []
    for j in range(n_chunk):
        panels = exchange(own_chunks[j], gate)
        gate = panels[:2]
        density_panels.append(panels)
    squares, rounded = [], []
    for j in range(n_chunk):
        across, along, top, bottom = density_panels[j]
        total, low = run([0, 1, 2, 3], panels=[[own_chunks[j]], [across], [along], [top, bottom]], rounded=True)
        squares.append(total)
        rounded.append(low)
    square_panels = []
    for j in range(n_chunk):
        panels = exchange(rounded[j], gate)
        gate = panels[:2]
        square_panels.append(panels)
    out = (rows, width)
    for j in range(n_chunk):
        across, along, top, bottom = square_panels[j]
        total = run([0, 1, 2], panels=[[rounded[j]], [across], [along]])
        out = run([3], panels=[[top, bottom]], total=total, square=squares[j], out=out, column=j)
    return out.reshape(rows, 1, width)


def solution(mesh):
    return jax.shard_map(
        shards,
        mesh=mesh,
        in_specs=(P("row", "col"), P(), P()),
        out_specs=P("row", "layer", "col"),
        check_vma=False,
    )
```

time: 1010 us -> 360 us (0.36)
  waiting for transfers between devices: 743 us -> 127 us
  Pallas kernels: 0 us -> 187 us
  local copies, waits for them, and re-layouts: 148 us -> 18.5 us
  matrix products: 83.5 us -> 0 us
  starting transfers between devices: 0.35 us -> 21.7 us
  other arithmetic: 19.4 us -> 1.5 us
  between operations: 13.2 us -> 0.15 us
    reduce_scatter x2 -> x0, waiting for transfers between devices: 561 us -> none  [the longest x1 281 us: shards(): lax.psum_scatter(partial_cube.astype(jnp.bfloat16), 'layer', scatter_dime...]
    pallas_call x0 -> x8, Pallas kernels: none -> 187 us  [the longest x6 177 us: product(): pl.pallas_call(functools.partial(product_kernel, plan, n_src, [len(g) for...]
    all_gather x3 -> x0, waiting for transfers between devices: 182 us -> none  [the longest x1 160 us: shards(): col_panel = lax.all_gather(own_rows, 'row', axis=0, tiled=True)]
    ppermute x0 -> x17, waiting for transfers between devices: none -> 127 us  [swap(): return lax.ppermute(x, axis, [(i, i ^ distance) for i in range(size)])]
    dot_general x2 -> x0, matrix products: 83.5 us -> none  [add_product(): return jnp.dot(segment, col_panel, preferred_element_type=jnp.float32)]
    reshape x3 -> x1, local copies, waits for them, and re-layouts: 73.4 us -> 0.1 us  [shards(): row_mask.reshape(block_rows // TILE, TILE, n_block // STEP, STEP)]
    transpose x2 -> x0, local copies, waits for them, and re-layouts: 53 us -> none  [shards(): regrouped = tile_here.reshape(block_rows, B, block_cols // layers, layers...]
    ppermute x0 -> x17, starting transfers between devices: none -> 21.7 us  [swap(): return lax.ppermute(x, axis, [(i, i ^ distance) for i in range(size)])]
  transfers between devices with their start and end apart: 5 -> 17, of which waited for: 4 -> 6; matrix products, arithmetic and copies ran while one was open for 3% -> 4% of each run, Pallas kernels for 0% -> 48%
where the time goes in v1:
time: 360 us; the launch traced here: 355 us
  Pallas kernels  187 us (52%)
  waiting for transfers between devices  127 us (35%)
  starting transfers between devices  21.7 us (6%)
  local copies, waits for them, and re-layouts  18.5 us (5%)
    pallas_call x6, Pallas kernels, product(): pl.pallas_call(functools.partial(product_kernel, plan, n_src, [len(g) for...  177 us
    ppermute x17, waiting for transfers between devices, swap(): return lax.ppermute(x, axis, [(i, i ^ distance) for i in range(size)])  127 us
    ppermute x17, starting transfers between devices, swap(): return lax.ppermute(x, axis, [(i, i ^ distance) for i in range(size)])  21.7 us
    pallas_call x2, Pallas kernels, pick_columns(): pl.pallas_call(functools.partial(pick_kernel, start), grid_spec=pltpu.Pre...  9.59 us
  transfers between devices with their start and end apart: 17, of which 6 were waited for; matrix products, arithmetic and copies ran while one was open for 4% of the time, Pallas kernels for 48%

profile of v1, /device:TPU:0, one launch (start us, length us, event | category | flops | bytes accessed | tf_op | source)
XLA Modules:
  0.0 355.2 jit_solution(10393517294556211519)
XLA Ops:
  2.0 4.8 %pick_columns.3.refs_12_ = bf16[2048,512]{1,0:T(8,128)(2,1)} custom-call(s32[1]{0:T(128)} %bitcast.14.where, s32[16,8]{1,0:T(8,128)} %copy.15.keep, bf16[2048,4096]{1,0:T(8,128)(2,1)} %refs_0_.11), custom_call_target="tpu_custom_call" | custom-call | tf_op jit(solution)/shard_map/pick_columns/pallas_call | solution.py:46
  6.8 2.5 collective-permute-start.2
  9.3 1.5 collective-permute-start.1
  10.8 4.8 %pick_columns.2.refs_12_ = bf16[2048,512]{1,0:T(8,128)(2,1)} custom-call(s32[1]{0:T(128)} %bitcast.14.where, s32[16,8]{1,0:T(8,128)} %copy.15.keep, bf16[2048,4096]{1,0:T(8,128)(2,1)} %refs_0_.11), custom_call_target="tpu_custom_call" | custom-call | tf_op jit(solution)/shard_map/pick_columns/pallas_call | solution.py:46
  15.6 40.3 %collective-permute-done.2.refs_14_ = bf16[2048,512]{1,0:T(8,128)(2,1)S(1)} collective-permute-done((bf16[2048,512]{1,0:T(8,128)(2,1)}, bf16[2048,512]{1,0:T(8,128)(2,1)S(1)}, u32[]{:S(2)}, u32[]{:S(2)}) %collective-permute-start.2) | collective-permute-done | bytes 2097184 | tf_op jit(solution)/shard_map/ppermute | solution.py:18
  55.9 1.5 collective-permute-done.1.refs_13_
  57.7 1.7 collective-permute-start.3
  61.9 1.7 collective-permute-start.7
  68.5 37.6 %collective-permute-done.4.refs_14_ = bf16[2048,512]{1,0:T(8,128)(2,1)S(1)} collective-permute-done((bf16[2048,512]{1,0:T(8,128)(2,1)}, bf16[2048,512]{1,0:T(8,128)(2,1)S(1)}, u32[]{:S(2)}, u32[]{:S(2)}) %collective-permute-start.4) | collective-permute-done | bytes 2097184 | tf_op jit(solution)/shard_map/ppermute | solution.py:18
  106.2 1.6 collective-permute-start.6
  107.7 2.3 slice.32
  110.5 18.5 %collective-permute-done.8.refs_16_ = bf16[1024,512]{1,0:T(8,128)(2,1)} collective-permute-done((bf16[1024,512]{1,0:T(8,128)(2,1)}, bf16[1024,512]{1,0:T(8,128)(2,1)}, u32[]{:S(2)}, u32[]{:S(2)}) %collective-permute-start.8) | collective-permute-done | bytes 1048608 | tf_op jit(solution)/shard_map/ppermute | solution.py:18
  129.0 41.9 %product.7 = (f32[2048,512]{1,0:T(8,128)}, bf16[2048,512]{1,0:T(8,128)(2,1)}) custom-call(s32[12]{0:T(128)} %stack.67.meta, s32[8,16]{1,0:T(8,128)} %reduce_max.9.active, s32[16,8]{1,0:T(8,128)} %copy.22.keep, bf16[2048,4096]{1,0:T(8,128)(2,1)} %refs_0_.11, bf16[2048,4096]{1,0:T(8,128)(2,1)} %collective-permute-done.refs_1_.refs_3_.refs_5_.refs_7_, ...), custom_call_target="tpu_custom_call" | custom-call | flops 17179869184 | bytes 33554432 | tf_op jit(solution)/shard_map/product/pallas_call | solution.py:157
  170.9 1.5 collective-permute-start.10
  172.4 3.0 collective-permute-start.9
  177.4 41.7 %product.6 = (f32[2048,512]{1,0:T(8,128)}, bf16[2048,512]{1,0:T(8,128)(2,1)}) custom-call(s32[12]{0:T(128)} %stack.67.meta, s32[8,16]{1,0:T(8,128)} %reduce_max.9.active, s32[16,8]{1,0:T(8,128)} %copy.22.keep, bf16[2048,4096]{1,0:T(8,128)(2,1)} %refs_0_.11, bf16[2048,4096]{1,0:T(8,128)(2,1)} %collective-permute-done.refs_1_.refs_3_.refs_5_.refs_7_, ...), custom_call_target="tpu_custom_call" | custom-call | flops 17179869184 | bytes 33554432 | tf_op jit(solution)/shard_map/product/pallas_call | solution.py:157
  220.5 1.4 collective-permute-start.11
  224.7 2.0 collective-permute-start.15
  226.7 31.1 %product.9.refs_5_ = f32[2048,512]{1,0:T(8,128)} custom-call(s32[12]{0:T(128)} %stack.67.meta, s32[8,16]{1,0:T(8,128)} %reduce_max.9.active, s32[16,8]{1,0:T(8,128)} %copy.22.keep, bf16[2048,4096]{1,0:T(8,128)(2,1)} %refs_0_.11, bf16[2048,4096]{1,0:T(8,128)(2,1)} %collective-permute-done.refs_1_.refs_3_.refs_5_.refs_7_, bf16[2048,4096]{1,0:T(8,128)(2,1)} %refs_0_.11, ...), custom_call_target="tpu_custom_call" | custom-call | flops 12884901888 | bytes 25165824 | tf_op jit(solution)/shard_map/product/pallas_call | solution.py:157
  257.8 28.6 %collective-permute-done.16.refs_4_ = bf16[1024,512]{1,0:T(8,128)(2,1)S(1)} collective-permute-done((bf16[1024,512]{1,0:T(8,128)(2,1)}, bf16[1024,512]{1,0:T(8,128)(2,1)S(1)}, u32[]{:S(2)}, u32[]{:S(2)}) %collective-permute-start.16) | collective-permute-done | bytes 1048608 | tf_op jit(solution)/shard_map/ppermute | solution.py:18
  287.4 15.7 %product.10.refs_7_ = bf16[2048,1024]{1,0:T(8,128)(2,1)} custom-call(s32[12]{0:T(128)} %stack.67.meta, s32[8,16]{1,0:T(8,128)} %reduce_max.9.active, s32[16,8]{1,0:T(8,128)} %copy.22.keep, bf16[2048,4096]{1,0:T(8,128)(2,1)} %refs_0_.11, bf16[2048,4096]{1,0:T(8,128)(2,1)} %collective-permute-done.refs_1_.refs_3_.refs_5_.refs_7_, ...), custom_call_target="tpu_custom_call" | custom-call | flops 4294967296 | bytes 8388608 | tf_op jit(solution)/shard_map/product/pallas_call | solution.py:157
  303.2 1.8 collective-permute-start.14
  306.9 31.2 %product.8.refs_5_ = f32[2048,512]{1,0:T(8,128)} custom-call(s32[12]{0:T(128)} %stack.67.meta, s32[8,16]{1,0:T(8,128)} %reduce_max.9.active, s32[16,8]{1,0:T(8,128)} %copy.22.keep, bf16[2048,4096]{1,0:T(8,128)(2,1)} %refs_0_.11, bf16[2048,4096]{1,0:T(8,128)(2,1)} %collective-permute-done.refs_1_.refs_3_.refs_5_.refs_7_, bf16[2048,4096]{1,0:T(8,128)(2,1)} %refs_0_.11, ...), custom_call_target="tpu_custom_call" | custom-call | flops 12884901888 | bytes 25165824 | tf_op jit(solution)/shard_map/product/pallas_call | solution.py:157
  339.5 15.7 %product.11 = bf16[2048,1024]{1,0:T(8,128)(2,1)} custom-call(s32[12]{0:T(128)} %stack.67.meta, s32[8,16]{1,0:T(8,128)} %reduce_max.9.active, s32[16,8]{1,0:T(8,128)} %copy.22.keep, bf16[2048,4096]{1,0:T(8,128)(2,1)} %refs_0_.11, bf16[2048,4096]{1,0:T(8,128)(2,1)} %collective-permute-done.refs_1_.refs_3_.refs_5_.refs_7_, ...), custom_call_target="tpu_custom_call", output_to_operand_aliasing={{}: (10, {})} | custom-call | flops 4294967296 | bytes 8388608 | tf_op jit(solution)/shard_map/product/pallas_call | solution.py:157
  (66 shorter events, 20.9 us)
Async XLA Ops:
  0.0 129.0 %collective-permute-start = (bf16[2048,4096]{1,0:T(8,128)(2,1)}, bf16[2048,4096]{1,0:T(8,128)(2,1)}, u32[]{:S(2)}, u32[]{:S(2)}) collective-permute-start(bf16[2048,4096]{1,0:T(8,128)(2,1)} %refs_0_.11), channel_id=1, source_target_pairs={{0,4},{4,0},{1,5},{5,1},{2,6},{6,2},{3,7},{7,3},{8,12},{12,8},{9,1... | collective-permute-start | bytes 50331656 | tf_op jit(solution)/shard_map/ppermute | solution.py:18
  6.8 49.0 %collective-permute-start.2 = (bf16[2048,512]{1,0:T(8,128)(2,1)}, bf16[2048,512]{1,0:T(8,128)(2,1)S(1)}, u32[]{:S(2)}, u32[]{:S(2)}) collective-permute-start(bf16[2048,512]{1,0:T(8,128)(2,1)} %pick_columns.3.refs_12_), channel_id=1, source_target_pairs={{0,16},{8,24},{16,0},{24,8},{1,17},{9,25},{17,1},{25,9},{2,18},{10... | collective-permute-start | bytes 6291464 | tf_op jit(solution)/shard_map/ppermute | solution.py:18
  9.3 48.0 %collective-permute-start.1 = (bf16[2048,512]{1,0:T(8,128)(2,1)}, bf16[2048,512]{1,0:T(8,128)(2,1)S(1)}, u32[]{:S(2)}, u32[]{:S(2)}) collective-permute-start(bf16[2048,512]{1,0:T(8,128)(2,1)} %pick_columns.3.refs_12_), channel_id=1, source_target_pairs={{0,8},{8,0},{16,24},{24,16},{1,9},{9,1},{17,25},{25,17},{2,10},{10... | collective-permute-start | bytes 6291464 | tf_op jit(solution)/shard_map/ppermute | solution.py:18
  55.8 6.0 %copy-start.1 = (bf16[2048,512]{1,0:T(8,128)(2,1)}, bf16[2048,512]{1,0:T(8,128)(2,1)S(1)}, u32[]{:S(2)}) copy-start(bf16[2048,512]{1,0:T(8,128)(2,1)S(1)} %collective-permute-done.2.refs_14_) | copy-start | bytes 6291460
  57.3 4.5 %copy-start.2 = (bf16[2048,512]{1,0:T(8,128)(2,1)}, bf16[2048,512]{1,0:T(8,128)(2,1)S(1)}, u32[]{:S(2)}) copy-start(bf16[2048,512]{1,0:T(8,128)(2,1)S(1)} %collective-permute-done.1.refs_13_) | copy-start | bytes 6291460
  57.3 48.8 %collective-permute-start.4 = (bf16[2048,512]{1,0:T(8,128)(2,1)}, bf16[2048,512]{1,0:T(8,128)(2,1)S(1)}, u32[]{:S(2)}, u32[]{:S(2)}) collective-permute-start(bf16[2048,512]{1,0:T(8,128)(2,1)} %pick_columns.2.refs_12_), channel_id=1, source_target_pairs={{0,16},{8,24},{16,0},{24,8},{1,17},{9,25},{17,1},{25,9},{2,18},{10... | collective-permute-start | bytes 6291464 | tf_op jit(solution)/shard_map/ppermute | solution.py:18
  57.7 50.1 %collective-permute-start.3 = (bf16[2048,512]{1,0:T(8,128)(2,1)}, bf16[2048,512]{1,0:T(8,128)(2,1)}, u32[]{:S(2)}, u32[]{:S(2)}) collective-permute-start(bf16[2048,512]{1,0:T(8,128)(2,1)} %pick_columns.2.refs_12_), channel_id=1, source_target_pairs={{0,8},{8,0},{16,24},{24,16},{1,9},{9,1},{17,25},{25,17},{2,10},{10... | collective-permute-start | bytes 6291464 | tf_op jit(solution)/shard_map/ppermute | solution.py:18
  60.4 68.6 %collective-permute-start.8 = (bf16[1024,512]{1,0:T(8,128)(2,1)}, bf16[1024,512]{1,0:T(8,128)(2,1)}, u32[]{:S(2)}, u32[]{:S(2)}) collective-permute-start(bf16[1024,512]{1,0:T(8,128)(2,1)} %slice.35), channel_id=1, source_target_pairs={{0,8},{8,0},{16,24},{24,16},{1,9},{9,1},{17,25},{25,17},{2,10},{10... | collective-permute-start | bytes 3145736 | tf_op jit(solution)/shard_map/ppermute | solution.py:18
  61.9 67.2 %collective-permute-start.7 = (bf16[1024,512]{1,0:T(8,128)(2,1)}, bf16[1024,512]{1,0:T(8,128)(2,1)}, u32[]{:S(2)}, u32[]{:S(2)}) collective-permute-start(bf16[1024,512]{1,0:T(8,128)(2,1)} %slice.34), channel_id=1, source_target_pairs={{0,16},{8,24},{16,0},{24,8},{1,17},{9,25},{17,1},{25,9},{2,18},{10... | collective-permute-start | bytes 3145736 | tf_op jit(solution)/shard_map/ppermute | solution.py:18
  106.1 3.9 %copy-start = (bf16[2048,512]{1,0:T(8,128)(2,1)}, bf16[2048,512]{1,0:T(8,128)(2,1)S(1)}, u32[]{:S(2)}) copy-start(bf16[2048,512]{1,0:T(8,128)(2,1)S(1)} %collective-permute-done.4.refs_14_) | copy-start | bytes 6291460
  106.2 69.3 %collective-permute-start.6 = (bf16[1024,512]{1,0:T(8,128)(2,1)S(1)}, bf16[1024,512]{1,0:T(8,128)(2,1)S(1)}, u32[]{:S(2)}, u32[]{:S(2)}) collective-permute-start(bf16[1024,512]{1,0:T(8,128)(2,1)S(1)} %slice.33), channel_id=1, source_target_pairs={{0,8},{8,0},{16,24},{24,16},{1,9},{9,1},{17,25},{25,17},{2,10},{10... | collective-permute-start | bytes 3145736 | tf_op jit(solution)/shard_map/ppermute | solution.py:18
  110.0 65.4 %collective-permute-start.5 = (bf16[1024,512]{1,0:T(8,128)(2,1)}, bf16[1024,512]{1,0:T(8,128)(2,1)S(1)}, u32[]{:S(2)}, u32[]{:S(2)}) collective-permute-start(bf16[1024,512]{1,0:T(8,128)(2,1)} %slice.32), channel_id=1, source_target_pairs={{0,16},{8,24},{16,0},{24,8},{1,17},{9,25},{17,1},{25,9},{2,18},{10... | collective-permute-start | bytes 3145736 | tf_op jit(solution)/shard_map/ppermute | solution.py:18
  170.9 48.2 %collective-permute-start.10 = (bf16[2048,512]{1,0:T(8,128)(2,1)}, bf16[2048,512]{1,0:T(8,128)(2,1)S(1)}, u32[]{:S(2)}, u32[]{:S(2)}) collective-permute-start(bf16[2048,512]{1,0:T(8,128)(2,1)} %get-tuple-element.15.refs_9_), channel_id=1, source_target_pairs={{0,16},{8,24},{16,0},{24,8},{1,17},{9,25},{17,1},{25,9},{2,18},{10... | collective-permute-start | bytes 6291464 | tf_op jit(solution)/shard_map/ppermute | solution.py:18
  172.4 46.7 %collective-permute-start.9 = (bf16[2048,512]{1,0:T(8,128)(2,1)}, bf16[2048,512]{1,0:T(8,128)(2,1)S(1)}, u32[]{:S(2)}, u32[]{:S(2)}) collective-permute-start(bf16[2048,512]{1,0:T(8,128)(2,1)} %get-tuple-element.15.refs_9_), channel_id=1, source_target_pairs={{0,8},{8,0},{16,24},{24,16},{1,9},{9,1},{17,25},{25,17},{2,10},{10... | collective-permute-start | bytes 6291464 | tf_op jit(solution)/shard_map/ppermute | solution.py:18
  219.2 5.5 %copy-start.5 = (bf16[2048,512]{1,0:T(8,128)(2,1)}, bf16[2048,512]{1,0:T(8,128)(2,1)S(1)}, u32[]{:S(2)}) copy-start(bf16[2048,512]{1,0:T(8,128)(2,1)S(1)} %collective-permute-done.10.refs_11_) | copy-start | bytes 6291460
  220.5 3.1 copy-start.7
  220.5 82.6 %collective-permute-start.13 = (bf16[2048,512]{1,0:T(8,128)(2,1)}, bf16[2048,512]{1,0:T(8,128)(2,1)S(1)}, u32[]{:S(2)}, u32[]{:S(2)}) collective-permute-start(bf16[2048,512]{1,0:T(8,128)(2,1)} %get-tuple-element.16.refs_9_), channel_id=1, source_target_pairs={{0,16},{8,24},{16,0},{24,8},{1,17},{9,25},{17,1},{25,9},{2,18},{10... | collective-permute-start | bytes 6291464 | tf_op jit(solution)/shard_map/ppermute | solution.py:18
  220.5 84.5 %collective-permute-start.11 = (bf16[2048,512]{1,0:T(8,128)(2,1)}, bf16[2048,512]{1,0:T(8,128)(2,1)S(1)}, u32[]{:S(2)}, u32[]{:S(2)}) collective-permute-start(bf16[2048,512]{1,0:T(8,128)(2,1)} %get-tuple-element.16.refs_9_), channel_id=1, source_target_pairs={{0,8},{8,0},{16,24},{24,16},{1,9},{9,1},{17,25},{25,17},{2,10},{10... | collective-permute-start | bytes 6291464 | tf_op jit(solution)/shard_map/ppermute | solution.py:18
  223.0 63.4 %collective-permute-start.16 = (bf16[1024,512]{1,0:T(8,128)(2,1)}, bf16[1024,512]{1,0:T(8,128)(2,1)S(1)}, u32[]{:S(2)}, u32[]{:S(2)}) collective-permute-start(bf16[1024,512]{1,0:T(8,128)(2,1)} %slice.39), channel_id=1, source_target_pairs={{0,8},{8,0},{16,24},{24,16},{1,9},{9,1},{17,25},{25,17},{2,10},{10... | collective-permute-start | bytes 3145736 | tf_op jit(solution)/shard_map/ppermute | solution.py:18
  224.7 61.9 %collective-permute-start.15 = (bf16[1024,512]{1,0:T(8,128)(2,1)}, bf16[1024,512]{1,0:T(8,128)(2,1)}, u32[]{:S(2)}, u32[]{:S(2)}) collective-permute-start(bf16[1024,512]{1,0:T(8,128)(2,1)} %slice.38), channel_id=1, source_target_pairs={{0,16},{8,24},{16,0},{24,8},{1,17},{9,25},{17,1},{25,9},{2,18},{10... | collective-permute-start | bytes 3145736 | tf_op jit(solution)/shard_map/ppermute | solution.py:18
  303.2 3.0 copy-start.3
  303.2 34.9 %collective-permute-start.14 = (bf16[1024,512]{1,0:T(8,128)(2,1)S(1)}, bf16[1024,512]{1,0:T(8,128)(2,1)S(1)}, u32[]{:S(2)}, u32[]{:S(2)}) collective-permute-start(bf16[1024,512]{1,0:T(8,128)(2,1)S(1)} %slice.37), channel_id=1, source_target_pairs={{0,8},{8,0},{16,24},{24,16},{1,9},{9,1},{17,25},{25,17},{2,10},{10... | collective-permute-start | bytes 3145736 | tf_op jit(solution)/shard_map/ppermute | solution.py:18
  305.0 1.9 copy-start.4
  306.2 31.9 %collective-permute-start.12 = (bf16[1024,512]{1,0:T(8,128)(2,1)}, bf16[1024,512]{1,0:T(8,128)(2,1)S(1)}, u32[]{:S(2)}, u32[]{:S(2)}) collective-permute-start(bf16[1024,512]{1,0:T(8,128)(2,1)} %slice.36), channel_id=1, source_target_pairs={{0,16},{8,24},{16,0},{24,8},{1,17},{9,25},{17,1},{25,9},{2,18},{10... | collective-permute-start | bytes 3145736 | tf_op jit(solution)/shard_map/ppermute | solution.py:18
  (6 other events, 6.8 us)

commit v2 on v1

v2 whole, which is shorter than its diff:
```python
import functools

import jax
import jax.numpy as jnp
from jax import lax
from jax.experimental import pallas as pl
from jax.experimental.pallas import tpu as pltpu
from jax.sharding import PartitionSpec as P

B = 128
TILE = 2
VMEM = 56 * 2**20


def swap(x, axis, distance):
    size = lax.axis_size(axis)
    return lax.ppermute(x, axis, [(i, i ^ distance) for i in range(size)])


def after(x, *earlier):
    return lax.optimization_barrier((x, *earlier))[0]


class Exchange:
    def __init__(self, own, whole, *gate):
        self.own, self.whole = own, whole
        if gate:
            own = after(own, *gate)
        half = own.shape[0] // 2
        self.top, self.bottom = own[:half], own[half:]
        if whole:
            self.across, self.along = [swap(own, "row", 1)], [swap(own, "row", 2)]
            self.hops = self.across[0][:half], self.along[0][half:]
        else:
            self.hops = swap(self.top, "row", 1), swap(self.bottom, "row", 2)

    def second(self, *gate):
        if not self.whole:
            top, bottom = after(self.top, *gate), after(self.bottom, *gate)
            self.across = [self.hops[0], swap(bottom, "row", 1)]
            self.along = [swap(top, "row", 2), self.hops[1]]

    def relay(self, *gate):
        top, bottom = (after(x, *gate) if gate else x for x in self.hops)
        self.far = [swap(top, "row", 2), swap(bottom, "row", 1)]

    def near(self):
        return [[self.own], self.across, self.along]


def pick_kernel(start, where, keep, x_ref, o_ref):
    q = pl.program_id(0)
    for i in range(x_ref.shape[0] // B):
        kept = keep[i, start + q] != 0
        rows = pl.ds(i * B, B)
        block = x_ref[rows, :]
        o_ref[rows, :] = jnp.where(kept, block, jnp.zeros_like(block))


def pick_columns(density, keep, layer, layers, start, group):
    rows = density.shape[0]
    return pl.pallas_call(
        functools.partial(pick_kernel, start),
        grid_spec=pltpu.PrefetchScalarGridSpec(
            num_scalar_prefetch=2,
            grid=(group,),
            in_specs=[
                pl.BlockSpec((rows, B), lambda q, where, keep: (0, (start + q) * layers + where[0]))
            ],
            out_specs=pl.BlockSpec((rows, B), lambda q, where, keep: (0, q)),
        ),
        out_shape=jax.ShapeDtypeStruct((rows, group * B), density.dtype),
        compiler_params=pltpu.CompilerParams(vmem_limit_bytes=VMEM),
        name="pick_columns",
    )(jnp.reshape(layer, (1,)), keep, density)


def product_kernel(plan, pieces, full, first, last, column, meta, keep, *refs):
    refs = list(refs)
    take = lambda n: [refs.pop(0) for _ in range(n)]
    n_slot = meta.shape[0] // 3
    lhs, masks = take(n_slot), take(n_slot)
    panels = [take(n) for n in pieces]
    total_in = None if first else take(1)[0]
    square_in = take(1)[0] if last else None
    if last and column > 0:
        take(1)
    total, held, sems = refs[-3:]
    outs = refs[:-3]
    i = pl.program_id(0)
    tile = total.shape[0]
    depth = held.shape[0] // n_slot

    @pl.when(i == 0)
    def _():
        copies = []
        for p, m in enumerate(plan):
            for h, panel in enumerate(panels[p]):
                size = panel.shape[0]
                at = pl.multiple_of(meta[m] * depth + h * size, size)
                copies.append(pltpu.make_async_copy(
                    panel, held.at[pl.ds(at, size)], sems.at[len(copies)]))
        for copy in copies:
            copy.start()
        for copy in copies:
            copy.wait()

    total[...] = jnp.zeros_like(total) if first else total_in[...]
    for s in range(n_slot):
        def add():
            kept = [
                jnp.broadcast_to(masks[s][0, t:t + 1, :], (B, depth)) for t in range(tile // B)
            ]
            kept = jnp.concatenate(kept, axis=0).astype(jnp.bfloat16)
            total[...] += jnp.dot(
                lhs[s][...] * kept, held[pl.ds(s * depth, depth), :],
                preferred_element_type=jnp.float32)

        if full:
            add()
        else:
            pl.when(meta[2 * n_slot + s] != 0)(add)
    if not last:
        outs[0][...] = total[...]
        if len(outs) > 1:
            outs[1][...] = total[...].astype(jnp.bfloat16)
        return
    step = total.shape[1] // B
    for t in range(tile // B):
        for q in range(step):
            at = (pl.ds(t * B, B), pl.ds(q * B, B))
            value = 3.0 * square_in[at] - 2.0 * total[at]
            kept = keep[i * (tile // B) + t, column * step + q] != 0
            outs[0][at] = jnp.where(kept, value, 0.0).astype(outs[0].dtype)


def product(plan, slots, owners, keep, sources, mask, panels, total=None, rounded=False,
            square=None, out=None, column=0):
    rows = sources[0].shape[0]
    width = panels[0][0].shape[1]
    tile = TILE * B
    depth = rows
    steps = rows // tile
    n_slot = len(slots)
    per_source = n_slot // len(sources)
    first, last, full = total is None, square is not None, len(plan) == n_slot
    used = [sum((slots[m] == s).astype(jnp.int32) for m in plan) for s in range(n_slot)]
    meta = jnp.stack([*slots, *owners, *used])
    pieces = [len(group) for group in panels]
    specs, args = [], []
    for s in range(n_slot):
        def index(i, meta, keep, s=s):
            return i if full else jnp.where(meta[2 * n_slot + s] != 0, i, 0), s % per_source
        specs.append(pl.BlockSpec((tile, depth), index))
        args.append(sources[s // per_source])
    for s in range(n_slot):
        specs.append(
            pl.BlockSpec((1, TILE, depth), lambda i, meta, keep, s=s: (i, 0, meta[n_slot + s])))
        args.append(mask)
    for group in panels:
        for panel in group:
            specs.append(pl.BlockSpec(memory_space=pl.ANY))
            args.append(panel)
    row_block = pl.BlockSpec((tile, width), lambda i, *_: (i, 0))
    if not first:
        specs.append(row_block)
        args.append(total)
    aliases = {}
    if last:
        specs.append(row_block)
        args.append(square)
        if column > 0:
            specs.append(pl.BlockSpec(memory_space=pl.ANY))
            args.append(out)
            aliases = {2 + len(args) - 1: 0}
        out_shape = [jax.ShapeDtypeStruct(out if column == 0 else out.shape, jnp.bfloat16)]
        out_specs = [pl.BlockSpec((tile, width), lambda i, *_: (i, column))]
    else:
        out_shape = [jax.ShapeDtypeStruct((rows, width), jnp.float32)]
        out_specs = [row_block]
        if rounded:
            out_shape.append(jax.ShapeDtypeStruct((rows, width), jnp.bfloat16))
            out_specs.append(row_block)
    flops = 2 * rows * depth * len(plan) * width
    result = pl.pallas_call(
        functools.partial(product_kernel, plan, pieces, full, first, last, column),
        grid_spec=pltpu.PrefetchScalarGridSpec(
            num_scalar_prefetch=2,
            grid=(steps,),
            in_specs=specs,
            out_specs=out_specs,
            scratch_shapes=[
                pltpu.VMEM((tile, width), jnp.float32),
                pltpu.VMEM((n_slot * depth, width), jnp.bfloat16),
                pltpu.SemaphoreType.DMA((sum(pieces),)),
            ],
        ),
        out_shape=out_shape,
        input_output_aliases=aliases,
        cost_estimate=pl.CostEstimate(
            flops=flops, bytes_accessed=2 * rows * depth * len(plan), transcendentals=0),
        compiler_params=pltpu.CompilerParams(vmem_limit_bytes=VMEM),
        name="product",
    )(meta, keep, *args)
    return result if rounded else result[0]


def shards(density, density_pattern, result_pattern):
    rows, cols = density.shape
    layers = lax.axis_size("layer")
    n_col = lax.axis_size("col")
    block_rows, block_cols = rows // B, cols // B
    group = block_cols // layers
    width = group * B
    r, c, l = (lax.axis_index(a) for a in ("row", "col", "layer"))
    n_chunk = 2 if group % 4 == 0 else 1
    chunk_w = width // n_chunk

    def pattern_tile(pattern):
        here = lax.dynamic_slice(pattern, (r * block_rows, c * block_cols), (block_rows, block_cols))
        return lax.dynamic_index_in_dim(here.reshape(block_rows, group, layers), l, 2, keepdims=False)

    if n_col == 2:
        sources = [density, swap(density, "col", 1)]
    else:
        sources = [lax.all_gather(density, "col", axis=1, tiled=True)]
    own_mask = pattern_tile(density_pattern)
    step = group // n_chunk
    own_chunks = [
        pick_columns(density, own_mask, l, layers, j * step, step) for j in range(n_chunk)
    ]
    row_mask = lax.dynamic_slice_in_dim(density_pattern, r * block_rows, block_rows, 0)
    n_block = row_mask.shape[1]
    mask = jnp.repeat(row_mask.astype(jnp.float32), B, axis=1)
    mask = mask.reshape(block_rows // TILE, TILE, n_block * B)
    keep = pattern_tile(result_pattern)
    n_slot = n_block * B // rows
    per_source = n_slot // len(sources)
    slots, owners = [], []
    for m in range(n_slot):
        owner = r ^ m
        source = (owner // per_source != c).astype(jnp.int32) if len(sources) == 2 else 0
        slots.append(source * per_source + owner % per_source)
        source = m // per_source
        owners.append((c ^ source) * per_source + m % per_source if len(sources) == 2 else jnp.int32(m))
    run = functools.partial(
        product, slots=slots, owners=owners, keep=keep, sources=sources, mask=mask)

    every = list(range(n_slot))
    near, far = every[:-1], every[-1:]

    def exchange(own, *early):
        first = Exchange(own[0], True)
        rest = [Exchange(x, False, *early) for x in own[1:]]
        first.relay(*early)
        total = run(near, panels=first.near())
        for x in rest:
            x.second(total)
            x.relay()
        return [first, *rest], total

    (first, *rest), total = exchange(own_chunks, *sources[1:])
    sums = [run(far, panels=[first.far], total=total, rounded=True)]
    sums += [run(every, panels=[*x.near(), x.far], rounded=True) for x in rest]
    (first, *rest), total = exchange([low for _, low in sums])
    totals = [total, *(run(near, panels=x.near()) for x in rest)]
    out = (rows, width)
    for j, x in enumerate([first, *rest]):
        out = run(far, panels=[x.far], total=totals[j], square=sums[j][0], out=out, column=j)
    return out.reshape(rows, 1, width)


def solution(mesh):
    return jax.shard_map(
        shards,
        mesh=mesh,
        in_specs=(P("row", "col"), P(), P()),
        out_specs=P("row", "layer", "col"),
        check_vma=False,
    )
```

time: 360 us -> 311 us (0.86); the launches traced: 355 us -> 310 us
  Pallas kernels: 187 us -> 160 us
  waiting for transfers between devices: 127 us -> 107 us
    pallas_call x6 -> x7, Pallas kernels: 177 us -> 150 us  [product(): pl.pallas_call(functools.partial(product_kernel, plan, pieces, full, firs...]
    ppermute x17 -> x21, waiting for transfers between devices: 127 us -> 107 us  [swap(): return lax.ppermute(x, axis, [(i, i ^ distance) for i in range(size)])]
    slice x8 -> x6, local copies, waits for them, and re-layouts: 7.84 us -> 10.3 us  [the longest x4 5.81 us: __init__(): self.hops = (self.across[0][:half], self.along[0][half:])]
    ppermute x17 -> x21, starting transfers between devices: 21.7 us -> 22.2 us  [swap(): return lax.ppermute(x, axis, [(i, i ^ distance) for i in range(size)])]
  transfers between devices with their start and end apart: 17 -> 21, of which waited for: 6 -> 11; matrix products, arithmetic and copies ran while one was open for 4% -> 6% of each run, Pallas kernels for 48% -> 47%
where the time goes in v2:
time: 311 us; the launch traced here: 310 us
  Pallas kernels  160 us (51%)
  waiting for transfers between devices  107 us (34%)
  starting transfers between devices  22.2 us (7%)
  local copies, waits for them, and re-layouts  19.9 us (6%)
    pallas_call x7, Pallas kernels, product(): pl.pallas_call(functools.partial(product_kernel, plan, pieces, full, firs...  150 us
    ppermute x21, waiting for transfers between devices, swap(): return lax.ppermute(x, axis, [(i, i ^ distance) for i in range(size)])  107 us
    ppermute x21, starting transfers between devices, swap(): return lax.ppermute(x, axis, [(i, i ^ distance) for i in range(size)])  22.2 us
    pallas_call x2, Pallas kernels, pick_columns(): pl.pallas_call(functools.partial(pick_kernel, start), grid_spec=pltpu.Pre...  9.7 us
  transfers between devices with their start and end apart: 21, of which 11 were waited for; matrix products, arithmetic and copies ran while one was open for 6% of the time, Pallas kernels for 47%

profile of v2, /device:TPU:0, one launch (start us, length us, event | category | flops | bytes accessed | tf_op | source)
XLA Modules:
  0.0 309.9 jit_solution(11647010556680083238)
XLA Ops:
  2.0 4.8 %pick_columns.3.refs_8_ = bf16[2048,512]{1,0:T(8,128)(2,1)} custom-call(s32[1]{0:T(128)} %bitcast.18.where, s32[16,8]{1,0:T(8,128)} %copy.16.keep, bf16[2048,4096]{1,0:T(8,128)(2,1)} %refs_1_.13), custom_call_target="tpu_custom_call" | custom-call | tf_op jit(solution)/shard_map/pick_columns/pallas_call | solution.py:62
  6.8 2.5 collective-permute-start.2
  10.8 4.9 %pick_columns.2.refs_8_ = bf16[2048,512]{1,0:T(8,128)(2,1)} custom-call(s32[1]{0:T(128)} %bitcast.18.where, s32[16,8]{1,0:T(8,128)} %copy.16.keep, bf16[2048,4096]{1,0:T(8,128)(2,1)} %refs_1_.13), custom_call_target="tpu_custom_call" | custom-call | tf_op jit(solution)/shard_map/pick_columns/pallas_call | solution.py:62
  19.9 35.9 %collective-permute-done.2.refs_9_ = bf16[2048,512]{1,0:T(8,128)(2,1)S(1)} collective-permute-done((bf16[2048,512]{1,0:T(8,128)(2,1)}, bf16[2048,512]{1,0:T(8,128)(2,1)S(1)}, u32[]{:S(2)}, u32[]{:S(2)}) %collective-permute-start.2) | collective-permute-done | bytes 2097184 | tf_op jit(solution)/shard_map/ppermute | solution.py:17
  57.4 2.4 slice.33
  59.8 1.5 collective-permute-start.13
  65.3 25.3 %product.7.refs_10_ = f32[2048,512]{1,0:T(8,128)} custom-call(s32[12]{0:T(128)} %stack.68.meta, s32[16,8]{1,0:T(8,128)} %copy.24.keep, bf16[2048,4096]{1,0:T(8,128)(2,1)} %refs_1_.13, bf16[2048,4096]{1,0:T(8,128)(2,1)} %refs_1_.13, bf16[2048,4096]{1,0:T(8,128)(2,1)} %collective-permute-done.refs_2_.refs_3_, ...), custom_call_target="tpu_custom_call" | custom-call | flops 12884901888 | bytes 25165824 | tf_op jit(solution)/shard_map/product/pallas_call | solution.py:185
  90.6 1.6 collective-permute-start.5
  93.3 16.8 %collective-permute-done.1.refs_9_ = bf16[1024,512]{1,0:T(8,128)(2,1)S(1)} collective-permute-done((bf16[1024,512]{1,0:T(8,128)(2,1)}, bf16[1024,512]{1,0:T(8,128)(2,1)S(1)}, u32[]{:S(2)}, u32[]{:S(2)}) %collective-permute-start.1) | collective-permute-done | bytes 1048608 | tf_op jit(solution)/shard_map/ppermute | solution.py:17
  113.2 15.5 %product.9 = (f32[2048,512]{1,0:T(8,128)}, bf16[2048,512]{1,0:T(8,128)(2,1)}) custom-call(s32[12]{0:T(128)} %stack.58.meta, s32[16,8]{1,0:T(8,128)} %copy.24.keep, bf16[2048,4096]{1,0:T(8,128)(2,1)} %refs_1_.13, bf16[2048,4096]{1,0:T(8,128)(2,1)} %refs_1_.13, bf16[2048,4096]{1,0:T(8,128)(2,1)} %collective-permute-done.refs_2_.refs_3_, ...), custom_call_target="tpu_custom_call" | custom-call | flops 4294967296 | bytes 8388608 | tf_op jit(solution)/shard_map/product/pallas_call | solution.py:185
  133.0 20.3 %collective-permute-done.7.refs_13_ = bf16[1024,512]{1,0:T(8,128)(2,1)} collective-permute-done((bf16[1024,512]{1,0:T(8,128)(2,1)S(1)}, bf16[1024,512]{1,0:T(8,128)(2,1)}, u32[]{:S(2)}, u32[]{:S(2)}) %collective-permute-start.7) | collective-permute-done | bytes 1048608 | tf_op jit(solution)/shard_map/ppermute | solution.py:17
  153.4 1.7 collective-permute-done.8.refs_14_
  155.1 27.2 %product.8 = (f32[2048,512]{1,0:T(8,128)}, bf16[2048,512]{1,0:T(8,128)(2,1)}) custom-call(s32[12]{0:T(128)} %stack.63.meta, s32[16,8]{1,0:T(8,128)} %copy.24.keep, bf16[2048,4096]{1,0:T(8,128)(2,1)} %refs_1_.13, bf16[2048,4096]{1,0:T(8,128)(2,1)} %refs_1_.13, bf16[2048,4096]{1,0:T(8,128)(2,1)} %collective-permute-done.refs_2_.refs_3_, ...), custom_call_target="tpu_custom_call" | custom-call | flops 17179869184 | bytes 33554432 | tf_op jit(solution)/shard_map/product/pallas_call | solution.py:185
  182.3 3.0 fusion
  186.8 13.2 %collective-permute-done.15.refs_9_ = bf16[2048,512]{1,0:T(8,128)(2,1)S(1)} collective-permute-done((bf16[2048,512]{1,0:T(8,128)(2,1)}, bf16[2048,512]{1,0:T(8,128)(2,1)S(1)}, u32[]{:S(2)}, u32[]{:S(2)}) %collective-permute-start.15) | collective-permute-done | bytes 2097184 | tf_op jit(solution)/shard_map/ppermute | solution.py:17
  201.6 2.3 slice.35
  204.8 25.3 %product.10.refs_10_ = f32[2048,512]{1,0:T(8,128)} custom-call(s32[12]{0:T(128)} %stack.68.meta, s32[16,8]{1,0:T(8,128)} %copy.24.keep, bf16[2048,4096]{1,0:T(8,128)(2,1)} %refs_1_.13, bf16[2048,4096]{1,0:T(8,128)(2,1)} %refs_1_.13, bf16[2048,4096]{1,0:T(8,128)(2,1)} %collective-permute-done.refs_2_.refs_3_, ...), custom_call_target="tpu_custom_call" | custom-call | flops 12884901888 | bytes 25165824 | tf_op jit(solution)/shard_map/product/pallas_call | solution.py:185
  230.1 1.6 collective-permute-start.18
  233.3 9.9 %collective-permute-done.19.refs_8_ = bf16[1024,512]{1,0:T(8,128)(2,1)S(1)} collective-permute-done((bf16[1024,512]{1,0:T(8,128)(2,1)}, bf16[1024,512]{1,0:T(8,128)(2,1)S(1)}, u32[]{:S(2)}, u32[]{:S(2)}) %collective-permute-start.19) | collective-permute-done | bytes 1048608 | tf_op jit(solution)/shard_map/ppermute | solution.py:17
  245.9 15.8 %product.12.refs_12_ = bf16[2048,1024]{1,0:T(8,128)(2,1)} custom-call(s32[12]{0:T(128)} %stack.58.meta, s32[16,8]{1,0:T(8,128)} %copy.24.keep, bf16[2048,4096]{1,0:T(8,128)(2,1)} %refs_1_.13, bf16[2048,4096]{1,0:T(8,128)(2,1)} %refs_1_.13, bf16[2048,4096]{1,0:T(8,128)(2,1)} %collective-permute-done.refs_2_.refs_3_, ...), custom_call_target="tpu_custom_call" | custom-call | flops 4294967296 | bytes 8388608 | tf_op jit(solution)/shard_map/product/pallas_call | solution.py:185
  261.7 3.9 %collective-permute-done.18.refs_11_ = bf16[1024,512]{1,0:T(8,128)(2,1)S(1)} collective-permute-done((bf16[1024,512]{1,0:T(8,128)(2,1)}, bf16[1024,512]{1,0:T(8,128)(2,1)S(1)}, u32[]{:S(2)}, u32[]{:S(2)}) %collective-permute-start.18) | collective-permute-done | bytes 1048608 | tf_op jit(solution)/shard_map/ppermute | solution.py:17
  265.6 1.8 collective-permute-done.17.refs_10_
  267.5 25.3 %product.11.refs_10_ = f32[2048,512]{1,0:T(8,128)} custom-call(s32[12]{0:T(128)} %stack.68.meta, s32[16,8]{1,0:T(8,128)} %copy.24.keep, bf16[2048,4096]{1,0:T(8,128)(2,1)} %refs_1_.13, bf16[2048,4096]{1,0:T(8,128)(2,1)} %refs_1_.13, bf16[2048,4096]{1,0:T(8,128)(2,1)} %collective-permute-done.refs_2_.refs_3_, ...), custom_call_target="tpu_custom_call" | custom-call | flops 12884901888 | bytes 25165824 | tf_op jit(solution)/shard_map/product/pallas_call | solution.py:185
  294.1 15.7 %product.13 = bf16[2048,1024]{1,0:T(8,128)(2,1)} custom-call(s32[12]{0:T(128)} %stack.58.meta, s32[16,8]{1,0:T(8,128)} %copy.24.keep, bf16[2048,4096]{1,0:T(8,128)(2,1)} %refs_1_.13, bf16[2048,4096]{1,0:T(8,128)(2,1)} %refs_1_.13, bf16[2048,4096]{1,0:T(8,128)(2,1)} %collective-permute-done.refs_2_.refs_3_, ...), custom_call_target="tpu_custom_call", output_to_operand_aliasing={{}: (14, {})} | custom-call | flops 4294967296 | bytes 8388608 | tf_op jit(solution)/shard_map/product/pallas_call | solution.py:185
  (73 shorter events, 31.5 us)
Async XLA Ops:
  0.0 59.8 %collective-permute-start = (bf16[2048,4096]{1,0:T(8,128)(2,1)}, bf16[2048,4096]{1,0:T(8,128)(2,1)}, u32[]{:S(2)}, u32[]{:S(2)}) collective-permute-start(bf16[2048,4096]{1,0:T(8,128)(2,1)} %refs_1_.13), channel_id=1, source_target_pairs={{0,4},{4,0},{1,5},{5,1},{2,6},{6,2},{3,7},{7,3},{8,12},{12,8},{9,1... | collective-permute-start | bytes 50331656 | tf_op jit(solution)/shard_map/ppermute | solution.py:17
  6.8 49.0 %collective-permute-start.2 = (bf16[2048,512]{1,0:T(8,128)(2,1)}, bf16[2048,512]{1,0:T(8,128)(2,1)S(1)}, u32[]{:S(2)}, u32[]{:S(2)}) collective-permute-start(bf16[2048,512]{1,0:T(8,128)(2,1)} %pick_columns.3.refs_8_), channel_id=1, source_target_pairs={{0,8},{8,0},{16,24},{24,16},{1,9},{9,1},{17,25},{25,17},{2,10},{10... | collective-permute-start | bytes 6291464 | tf_op jit(solution)/shard_map/ppermute | solution.py:17
  9.3 48.1 %collective-permute-start.3 = (bf16[2048,512]{1,0:T(8,128)(2,1)}, bf16[2048,512]{1,0:T(8,128)(2,1)}, u32[]{:S(2)}, u32[]{:S(2)}) collective-permute-start(bf16[2048,512]{1,0:T(8,128)(2,1)} %pick_columns.3.refs_8_), channel_id=1, source_target_pairs={{0,16},{8,24},{16,0},{24,8},{1,17},{9,25},{17,1},{25,9},{2,18},{10... | collective-permute-start | bytes 6291464 | tf_op jit(solution)/shard_map/ppermute | solution.py:17
  19.9 42.3 %copy-start = (bf16[2048,512]{1,0:T(8,128)(2,1)S(1)}, bf16[2048,512]{1,0:T(8,128)(2,1)}, u32[]{:S(2)}) copy-start(bf16[2048,512]{1,0:T(8,128)(2,1)} %pick_columns.2.refs_8_) | copy-start | bytes 6291460
  59.8 32.4 %collective-permute-start.13 = (bf16[1024,512]{1,0:T(8,128)(2,1)S(1)}, bf16[1024,512]{1,0:T(8,128)(2,1)S(1)}, u32[]{:S(2)}, u32[]{:S(2)}) collective-permute-start(bf16[1024,512]{1,0:T(8,128)(2,1)S(1)} %slice.32), channel_id=1, source_target_pairs={{0,16},{8,24},{16,0},{24,8},{1,17},{9,25},{17,1},{25,9},{2,18},{10... | collective-permute-start | bytes 3145736 | tf_op jit(solution)/shard_map/ppermute | solution.py:17
  61.3 50.9 %collective-permute-start.14 = (bf16[1024,512]{1,0:T(8,128)(2,1)}, bf16[1024,512]{1,0:T(8,128)(2,1)S(1)}, u32[]{:S(2)}, u32[]{:S(2)}) collective-permute-start(bf16[1024,512]{1,0:T(8,128)(2,1)} %slice.33), channel_id=1, source_target_pairs={{0,8},{8,0},{16,24},{24,16},{1,9},{9,1},{17,25},{25,17},{2,10},{10... | collective-permute-start | bytes 3145736 | tf_op jit(solution)/shard_map/ppermute | solution.py:17
  63.7 46.4 %collective-permute-start.1 = (bf16[1024,512]{1,0:T(8,128)(2,1)}, bf16[1024,512]{1,0:T(8,128)(2,1)S(1)}, u32[]{:S(2)}, u32[]{:S(2)}) collective-permute-start(bf16[1024,512]{1,0:T(8,128)(2,1)} %get-tuple-element.18), channel_id=1, source_target_pairs={{0,8},{8,0},{16,24},{24,16},{1,9},{9,1},{17,25},{25,17},{2,10},{10... | collective-permute-start | bytes 3145736 | tf_op jit(solution)/shard_map/ppermute | solution.py:17
  64.8 45.8 %collective-permute-start.6 = (bf16[1024,512]{1,0:T(8,128)(2,1)}, bf16[1024,512]{1,0:T(8,128)(2,1)}, u32[]{:S(2)}, u32[]{:S(2)}) collective-permute-start(bf16[1024,512]{1,0:T(8,128)(2,1)} %get-tuple-element.17), channel_id=1, source_target_pairs={{0,16},{8,24},{16,0},{24,8},{1,17},{9,25},{17,1},{25,9},{2,18},{10... | collective-permute-start | bytes 3145736 | tf_op jit(solution)/shard_map/ppermute | solution.py:17
  90.6 40.3 %collective-permute-start.5 = (bf16[1024,512]{1,0:T(8,128)(2,1)}, bf16[1024,512]{1,0:T(8,128)(2,1)}, u32[]{:S(2)}, u32[]{:S(2)}) collective-permute-start(bf16[1024,512]{1,0:T(8,128)(2,1)} %get-tuple-element.18), channel_id=1, source_target_pairs={{0,16},{8,24},{16,0},{24,8},{1,17},{9,25},{17,1},{25,9},{2,18},{10... | collective-permute-start | bytes 3145736 | tf_op jit(solution)/shard_map/ppermute | solution.py:17
  92.2 40.8 %collective-permute-start.4 = (bf16[1024,512]{1,0:T(8,128)(2,1)}, bf16[1024,512]{1,0:T(8,128)(2,1)}, u32[]{:S(2)}, u32[]{:S(2)}) collective-permute-start(bf16[1024,512]{1,0:T(8,128)(2,1)} %get-tuple-element.17), channel_id=1, source_target_pairs={{0,8},{8,0},{16,24},{24,16},{1,9},{9,1},{17,25},{25,17},{2,10},{10... | collective-permute-start | bytes 3145736 | tf_op jit(solution)/shard_map/ppermute | solution.py:17
  110.1 43.3 %collective-permute-start.7 = (bf16[1024,512]{1,0:T(8,128)(2,1)S(1)}, bf16[1024,512]{1,0:T(8,128)(2,1)}, u32[]{:S(2)}, u32[]{:S(2)}) collective-permute-start(bf16[1024,512]{1,0:T(8,128)(2,1)S(1)} %collective-permute-done.1.refs_9_), channel_id=1, source_target_pairs={{0,16},{8,24},{16,0},{24,8},{1,17},{9,25},{17,1},{25,9},{2,18},{10... | collective-permute-start | bytes 3145736 | tf_op jit(solution)/shard_map/ppermute | solution.py:17
  110.6 44.5 %collective-permute-start.8 = (bf16[1024,512]{1,0:T(8,128)(2,1)}, bf16[1024,512]{1,0:T(8,128)(2,1)}, u32[]{:S(2)}, u32[]{:S(2)}) collective-permute-start(bf16[1024,512]{1,0:T(8,128)(2,1)} %collective-permute-done.6.refs_12_), channel_id=1, source_target_pairs={{0,8},{8,0},{16,24},{24,16},{1,9},{9,1},{17,25},{25,17},{2,10},{10... | collective-permute-start | bytes 3145736 | tf_op jit(solution)/shard_map/ppermute | solution.py:17
  128.7 71.2 %collective-permute-start.15 = (bf16[2048,512]{1,0:T(8,128)(2,1)}, bf16[2048,512]{1,0:T(8,128)(2,1)S(1)}, u32[]{:S(2)}, u32[]{:S(2)}) collective-permute-start(bf16[2048,512]{1,0:T(8,128)(2,1)} %get-tuple-element.22.refs_8_), channel_id=1, source_target_pairs={{0,8},{8,0},{16,24},{24,16},{1,9},{9,1},{17,25},{25,17},{2,10},{10... | collective-permute-start | bytes 6291464 | tf_op jit(solution)/shard_map/ppermute | solution.py:17
  130.9 70.7 %collective-permute-start.16 = (bf16[2048,512]{1,0:T(8,128)(2,1)}, bf16[2048,512]{1,0:T(8,128)(2,1)}, u32[]{:S(2)}, u32[]{:S(2)}) collective-permute-start(bf16[2048,512]{1,0:T(8,128)(2,1)} %get-tuple-element.22.refs_8_), channel_id=1, source_target_pairs={{0,16},{8,24},{16,0},{24,8},{1,17},{9,25},{17,1},{25,9},{2,18},{10... | collective-permute-start | bytes 6291464 | tf_op jit(solution)/shard_map/ppermute | solution.py:17
  185.3 46.4 %collective-permute-start.11 = (bf16[1024,512]{1,0:T(8,128)(2,1)}, bf16[1024,512]{1,0:T(8,128)(2,1)S(1)}, u32[]{:S(2)}, u32[]{:S(2)}) collective-permute-start(bf16[1024,512]{1,0:T(8,128)(2,1)} %get-tuple-element.23), channel_id=1, source_target_pairs={{0,16},{8,24},{16,0},{24,8},{1,17},{9,25},{17,1},{25,9},{2,18},{10... | collective-permute-start | bytes 3145736 | tf_op jit(solution)/shard_map/ppermute | solution.py:17
  185.8 47.1 %collective-permute-start.9 = (bf16[1024,512]{1,0:T(8,128)(2,1)}, bf16[1024,512]{1,0:T(8,128)(2,1)S(1)}, u32[]{:S(2)}, u32[]{:S(2)}) collective-permute-start(bf16[1024,512]{1,0:T(8,128)(2,1)} %get-tuple-element.24), channel_id=1, source_target_pairs={{0,8},{8,0},{16,24},{24,16},{1,9},{9,1},{17,25},{25,17},{2,10},{10... | collective-permute-start | bytes 3145736 | tf_op jit(solution)/shard_map/ppermute | solution.py:17
  201.0 42.1 %collective-permute-start.19 = (bf16[1024,512]{1,0:T(8,128)(2,1)}, bf16[1024,512]{1,0:T(8,128)(2,1)S(1)}, u32[]{:S(2)}, u32[]{:S(2)}) collective-permute-start(bf16[1024,512]{1,0:T(8,128)(2,1)} %slice.34), channel_id=1, source_target_pairs={{0,16},{8,24},{16,0},{24,8},{1,17},{9,25},{17,1},{25,9},{2,18},{10... | collective-permute-start | bytes 3145736 | tf_op jit(solution)/shard_map/ppermute | solution.py:17
  203.8 41.1 %collective-permute-start.20 = (bf16[1024,512]{1,0:T(8,128)(2,1)}, bf16[1024,512]{1,0:T(8,128)(2,1)S(1)}, u32[]{:S(2)}, u32[]{:S(2)}) collective-permute-start(bf16[1024,512]{1,0:T(8,128)(2,1)} %slice.35), channel_id=1, source_target_pairs={{0,8},{8,0},{16,24},{24,16},{1,9},{9,1},{17,25},{25,17},{2,10},{10... | collective-permute-start | bytes 3145736 | tf_op jit(solution)/shard_map/ppermute | solution.py:17
  230.1 35.5 %collective-permute-start.18 = (bf16[1024,512]{1,0:T(8,128)(2,1)}, bf16[1024,512]{1,0:T(8,128)(2,1)S(1)}, u32[]{:S(2)}, u32[]{:S(2)}) collective-permute-start(bf16[1024,512]{1,0:T(8,128)(2,1)} %get-tuple-element.24), channel_id=1, source_target_pairs={{0,16},{8,24},{16,0},{24,8},{1,17},{9,25},{17,1},{25,9},{2,18},{10... | collective-permute-start | bytes 3145736 | tf_op jit(solution)/shard_map/ppermute | solution.py:17
  231.7 30.0 %copy-start.4 = (bf16[1024,512]{1,0:T(8,128)(2,1)}, bf16[1024,512]{1,0:T(8,128)(2,1)S(1)}, u32[]{:S(2)}) copy-start(bf16[1024,512]{1,0:T(8,128)(2,1)S(1)} %collective-permute-done.11.refs_12_) | copy-start | bytes 3145732
  231.7 35.8 %collective-permute-start.17 = (bf16[1024,512]{1,0:T(8,128)(2,1)}, bf16[1024,512]{1,0:T(8,128)(2,1)}, u32[]{:S(2)}, u32[]{:S(2)}) collective-permute-start(bf16[1024,512]{1,0:T(8,128)(2,1)} %get-tuple-element.23), channel_id=1, source_target_pairs={{0,8},{8,0},{16,24},{24,16},{1,9},{9,1},{17,25},{25,17},{2,10},{10... | collective-permute-start | bytes 3145736 | tf_op jit(solution)/shard_map/ppermute | solution.py:17
  233.0 28.7 %copy-start.6 = (bf16[1024,512]{1,0:T(8,128)(2,1)}, bf16[1024,512]{1,0:T(8,128)(2,1)S(1)}, u32[]{:S(2)}) copy-start(bf16[1024,512]{1,0:T(8,128)(2,1)S(1)} %collective-permute-done.9.refs_9_) | copy-start | bytes 3145732
  233.0 59.8 %collective-permute-start.10 = (bf16[1024,512]{1,0:T(8,128)(2,1)S(1)}, bf16[1024,512]{1,0:T(8,128)(2,1)S(1)}, u32[]{:S(2)}, u32[]{:S(2)}) collective-permute-start(bf16[1024,512]{1,0:T(8,128)(2,1)S(1)} %collective-permute-done.9.refs_9_), channel_id=1, source_target_pairs={{0,16},{8,24},{16,0},{24,8},{1,17},{9,25},{17,1},{25,9},{2,18},{10... | collective-permute-start | bytes 3145736 | tf_op jit(solution)/shard_map/ppermute | solution.py:17
  243.1 49.6 %collective-permute-start.12 = (bf16[1024,512]{1,0:T(8,128)(2,1)S(1)}, bf16[1024,512]{1,0:T(8,128)(2,1)S(1)}, u32[]{:S(2)}, u32[]{:S(2)}) collective-permute-start(bf16[1024,512]{1,0:T(8,128)(2,1)S(1)} %collective-permute-done.11.refs_12_), channel_id=1, source_target_pairs={{0,8},{8,0},{16,24},{24,16},{1,9},{9,1},{17,25},{25,17},{2,10},{10... | collective-permute-start | bytes 3145736 | tf_op jit(solution)/shard_map/ppermute | solution.py:17
  (10 other events, 54.3 us)

commit v3 on v2

v3 whole, which is shorter than its diff:
```python
import functools

import jax
import jax.numpy as jnp
from jax import lax
from jax.experimental import pallas as pl
from jax.experimental.pallas import tpu as pltpu
from jax.sharding import PartitionSpec as P

B = 128
TILE = 2
VMEM = 62 * 2**20


def swap(x, axis, distance):
    size = lax.axis_size(axis)
    return lax.ppermute(x, axis, [(i, i ^ distance) for i in range(size)])


def after(x, *earlier):
    return lax.optimization_barrier((x, *earlier))[0]


class Exchange:
    def __init__(self, own, whole, *gate):
        self.own, self.whole = [own], whole
        if gate:
            own = after(own, *gate)
        half = own.shape[0] // 2
        self.top, self.bottom = own[:half], own[half:]
        if whole:
            self.across, self.along = [swap(own, "row", 1)], [swap(own, "row", 2)]
            self.hops = self.across[0][:half], self.along[0][half:]
        else:
            self.hops = swap(self.top, "row", 1), swap(self.bottom, "row", 2)

    def second(self, *gate):
        if not self.whole:
            top, bottom = after(self.top, *gate), after(self.bottom, *gate)
            self.across = [self.hops[0], swap(bottom, "row", 1)]
            self.along = [swap(top, "row", 2), self.hops[1]]

    def relay(self, *gate):
        top, bottom = (after(x, *gate) if gate else x for x in self.hops)
        self.far = [swap(top, "row", 2), swap(bottom, "row", 1)]

    def near(self):
        return [(0, self.own), (1, self.across), (2, self.along)]

    def early(self):
        return [(0, self.own), (1, [self.hops[0], None]), (2, [None, self.hops[1]])]

    def late(self):
        return [(1, [None, self.across[1]]), (2, [self.along[0], None])]


def pick_kernel(start, where, keep, *refs):
    *columns, o_ref = refs
    i = pl.program_id(0)
    step = o_ref.shape[0] // B
    for q, x_ref in enumerate(columns):
        for t in range(step):
            kept = keep[i * step + t, start + q] != 0
            block = x_ref[pl.ds(t * B, B), :]
            o_ref[pl.ds(t * B, B), pl.ds(q * B, B)] = jnp.where(kept, block, jnp.zeros_like(block))


def pick_columns(density, keep, layer, layers, start, group):
    rows = density.shape[0]
    tile = 2 * TILE * B

    def column(q):
        return pl.BlockSpec((tile, B), lambda i, where, keep: (i, (start + q) * layers + where[0]))

    return pl.pallas_call(
        functools.partial(pick_kernel, start),
        grid_spec=pltpu.PrefetchScalarGridSpec(
            num_scalar_prefetch=2,
            grid=(rows // tile,),
            in_specs=[column(q) for q in range(group)],
            out_specs=pl.BlockSpec((tile, group * B), lambda i, *_: (i, 0)),
        ),
        out_shape=jax.ShapeDtypeStruct((rows, group * B), density.dtype),
        compiler_params=pltpu.CompilerParams(vmem_limit_bytes=VMEM),
        name="pick_columns",
    )(jnp.reshape(layer, (1,)), keep, *[density] * group)


def product_kernel(plan, full, scale, meta, *refs):
    refs = list(refs)
    take = lambda n: [refs.pop(0) for _ in range(n)]
    n_slot = meta.shape[0] // 4
    lhs, masks = take(n_slot), take(n_slot)
    panels = [(m, at, take(1)[0]) for m, at in plan]
    base = take(1)[0] if scale else None
    total, held, sems = refs[-3:]
    outs = refs[:-3]
    i = pl.program_id(0)
    tile = total.shape[0]
    depth = held.shape[0] // n_slot

    @pl.when(i == 0)
    def _():
        copies = []
        for m, start, panel in panels:
            at = pl.multiple_of(meta[m] * depth + start, B)
            copies.append(pltpu.make_async_copy(
                panel, held.at[pl.ds(at, panel.shape[0])], sems.at[len(copies)]))
        for copy in copies:
            copy.start()
        for copy in copies:
            copy.wait()

    total[...] = jnp.zeros_like(total)
    whole = all(panel.shape[0] == depth for _, _, panel in panels)
    step = depth if full or whole else depth // 2
    for s in range(n_slot):
        for at in range(0, depth, step):
            def add():
                kept = [
                    jnp.broadcast_to(masks[s][0, t:t + 1, at:at + step], (B, step))
                    for t in range(tile // B)
                ]
                kept = jnp.concatenate(kept, axis=0).astype(jnp.bfloat16)
                total[...] += jnp.dot(
                    lhs[s][:, at:at + step] * kept, held[pl.ds(s * depth + at, step), :],
                    preferred_element_type=jnp.float32)

            if full:
                add()
            else:
                pl.when(meta[2 * n_slot + 2 * s + at // (depth // 2)] != 0)(add)
    if scale:
        outs[0][...] = scale * base[...] - 2.0 * total[...]
        return
    outs[0][...] = total[...]
    if len(outs) > 1:
        outs[1][...] = total[...].astype(jnp.bfloat16)


def far_kernel(column, meta, keep, first_ref, second_ref, mask, top, bottom, total_in, *outs):
    if column is not None:
        outs = outs[-1:]
    i = pl.program_id(0)
    tile, width = total_in.shape
    half = top.shape[0]

    def run(x_ref):
        kept = [jnp.broadcast_to(mask[0, t:t + 1, :], (B, 2 * half)) for t in range(tile // B)]
        x = x_ref[...] * jnp.concatenate(kept, axis=0).astype(jnp.bfloat16)
        part = jnp.dot(x[:, :half], top[...], preferred_element_type=jnp.float32)
        part = part + jnp.dot(x[:, half:], bottom[...], preferred_element_type=jnp.float32)
        if column is None:
            total = total_in[...] + part
            outs[0][...] = total
            outs[1][...] = total.astype(jnp.bfloat16)
            return
        value = total_in[...] - 2.0 * part
        for t in range(tile // B):
            for q in range(width // B):
                kept = keep[i * (tile // B) + t, column * (width // B) + q] != 0
                block = value[t * B:(t + 1) * B, q * B:(q + 1) * B]
                outs[0][pl.ds(t * B, B), pl.ds(q * B, B)] = (
                    jnp.where(kept, block, 0.0).astype(outs[0].dtype))

    pl.when(meta[0] == 0)(lambda: run(first_ref))
    pl.when(meta[0] == 1)(lambda: run(second_ref))


def far_product(slots, owners, keep, sources, mask, panels, total, out=None, column=None):
    rows, width = total.shape
    tile, depth = TILE * B, rows
    n_slot = len(slots)
    per_source = n_slot // len(sources)
    slot = slots[-1]
    owner = sum(jnp.where(slot == s, owners[s], 0) for s in range(n_slot))
    meta = jnp.stack([slot // per_source, slot % per_source, owner])
    if len(sources) == 1:
        sources = [sources[0], sources[0]]

    def rows_of(h):
        def index(i, meta, keep):
            here = meta[0] == h
            return jnp.where(here, i, 0), jnp.where(here, meta[1], 0)
        return pl.BlockSpec((tile, depth), index)

    panel = pl.BlockSpec(panels[0].shape, lambda i, *_: (0, 0), pipeline_mode=pl.Buffered(1))
    row_block = pl.BlockSpec((tile, width), lambda i, *_: (i, 0))
    specs = [
        rows_of(0), rows_of(1),
        pl.BlockSpec((1, TILE, depth), lambda i, meta, keep: (i, 0, meta[2])),
        panel, panel, row_block,
    ]
    args = [*sources, mask, *panels, total]
    aliases = {}
    if column is None:
        out_shape = [jax.ShapeDtypeStruct((rows, width), t) for t in (jnp.float32, jnp.bfloat16)]
        out_specs = [row_block, row_block]
    else:
        if column > 0:
            specs.append(pl.BlockSpec(memory_space=pl.ANY))
            args.append(out)
            aliases = {2 + len(args) - 1: 0}
        out_shape = [jax.ShapeDtypeStruct(out if column == 0 else out.shape, jnp.bfloat16)]
        out_specs = [pl.BlockSpec((tile, width), lambda i, *_: (i, column))]
    result = pl.pallas_call(
        functools.partial(far_kernel, column),
        grid_spec=pltpu.PrefetchScalarGridSpec(
            num_scalar_prefetch=2, grid=(rows // tile,), in_specs=specs, out_specs=out_specs),
        out_shape=out_shape,
        input_output_aliases=aliases,
        cost_estimate=pl.CostEstimate(
            flops=2 * rows * depth * width, bytes_accessed=2 * rows * depth, transcendentals=0),
        compiler_params=pltpu.CompilerParams(vmem_limit_bytes=VMEM),
        name="far_product",
    )(meta, keep, *args)
    return result if column is None else result[0]


def product(panels, slots, owners, sources, mask, rounded=False, base=None, scale=None):
    rows = sources[0].shape[0]
    width = next(x for x in panels[0][1] if x is not None).shape[1]
    plan, arrays, covers = [], [], []
    for m, pieces in panels:
        for h, x in enumerate(pieces):
            if x is not None:
                start = h * (rows // len(pieces))
                plan.append((m, start))
                arrays.append(x)
                covers += [(m, k) for k in range(2) if start <= k * (rows // 2) < start + x.shape[0]]
    tile = TILE * B
    depth = rows
    steps = rows // tile
    n_slot = len(slots)
    per_source = n_slot // len(sources)
    full = len(covers) == 2 * n_slot
    used = [
        sum(((slots[m] == s).astype(jnp.int32) for m, k in covers if k == h), jnp.int32(0))
        for s in range(n_slot) for h in range(2)
    ]
    meta = jnp.stack([*slots, *owners, *used])
    specs, args = [], []
    for s in range(n_slot):
        def index(i, meta, s=s):
            here = meta[2 * n_slot + 2 * s] + meta[2 * n_slot + 2 * s + 1] != 0
            return i if full else jnp.where(here, i, 0), s % per_source
        specs.append(pl.BlockSpec((tile, depth), index))
        args.append(sources[s // per_source])
    for s in range(n_slot):
        specs.append(
            pl.BlockSpec((1, TILE, depth), lambda i, meta, s=s: (i, 0, meta[n_slot + s])))
        args.append(mask)
    specs += [pl.BlockSpec(memory_space=pl.ANY)] * len(arrays)
    args += arrays
    row_block = pl.BlockSpec((tile, width), lambda i, *_: (i, 0))
    if base is not None:
        specs.append(row_block)
        args.append(base)
    out_shape = [jax.ShapeDtypeStruct((rows, width), jnp.float32)]
    out_specs = [row_block]
    if rounded:
        out_shape.append(jax.ShapeDtypeStruct((rows, width), jnp.bfloat16))
        out_specs.append(row_block)
    flops = rows * depth * len(covers) * width
    result = pl.pallas_call(
        functools.partial(product_kernel, plan, full, scale),
        grid_spec=pltpu.PrefetchScalarGridSpec(
            num_scalar_prefetch=1,
            grid=(steps,),
            in_specs=specs,
            out_specs=out_specs,
            scratch_shapes=[
                pltpu.VMEM((tile, width), jnp.float32),
                pltpu.VMEM((n_slot * depth, width), jnp.bfloat16),
                pltpu.SemaphoreType.DMA((len(arrays),)),
            ],
        ),
        out_shape=out_shape,
        cost_estimate=pl.CostEstimate(
            flops=flops, bytes_accessed=rows * depth * len(covers), transcendentals=0),
        compiler_params=pltpu.CompilerParams(vmem_limit_bytes=VMEM),
        name="product",
    )(meta, *args)
    return result if rounded else result[0]


def shards(density, density_pattern, result_pattern):
    rows, cols = density.shape
    layers = lax.axis_size("layer")
    n_col = lax.axis_size("col")
    block_rows, block_cols = rows // B, cols // B
    group = block_cols // layers
    width = group * B
    r, c, l = (lax.axis_index(a) for a in ("row", "col", "layer"))
    n_chunk = 2 if group % 4 == 0 else 1
    chunk_w = width // n_chunk

    def pattern_tile(pattern):
        here = lax.dynamic_slice(pattern, (r * block_rows, c * block_cols), (block_rows, block_cols))
        return lax.dynamic_index_in_dim(here.reshape(block_rows, group, layers), l, 2, keepdims=False)

    if n_col == 2:
        sources = [density, swap(density, "col", 1)]
    else:
        sources = [lax.all_gather(density, "col", axis=1, tiled=True)]
    own_mask = pattern_tile(density_pattern)
    step = group // n_chunk
    own_chunks = [
        pick_columns(density, own_mask, l, layers, j * step, step) for j in range(n_chunk)
    ]
    row_mask = lax.dynamic_slice_in_dim(density_pattern, r * block_rows, block_rows, 0)
    n_block = row_mask.shape[1]
    mask = jnp.repeat(row_mask.astype(jnp.float32), B, axis=1)
    mask = mask.reshape(block_rows // TILE, TILE, n_block * B)
    keep = pattern_tile(result_pattern)
    n_slot = n_block * B // rows
    per_source = n_slot // len(sources)
    slots, owners = [], []
    for m in range(n_slot):
        owner = r ^ m
        source = (owner // per_source != c).astype(jnp.int32) if len(sources) == 2 else 0
        slots.append(source * per_source + owner % per_source)
        source = m // per_source
        owners.append((c ^ source) * per_source + m % per_source if len(sources) == 2 else jnp.int32(m))
    common = dict(slots=slots, owners=owners, sources=sources, mask=mask)
    run = functools.partial(product, **common)
    run_far = functools.partial(far_product, keep=keep, **common)

    def exchange(own, early=(), **how):
        first = Exchange(own[0], True)
        rest = [Exchange(x, False) for x in own[1:]]
        first.relay(*early)
        first.own = [after(own[0], *first.hops)]
        total = run(first.near(), **how)
        for x in rest:
            x.second(total)
        return first, rest, total

    first, rest, total = exchange(own_chunks, sources[1:])
    for x in rest:
        x.relay(total)
    sums = [run_far(panels=first.far, total=total)]
    sums += [run([*x.near(), (n_slot - 1, x.far)], rounded=True) for x in rest]
    squares = [square for square, _ in sums]
    first, rest, total = exchange([low for _, low in sums], base=squares[0], scale=3.0)
    totals = [run(x.early(), base=y, scale=3.0) for x, y in zip(rest, squares[1:])]
    for x, y in zip(rest, totals):
        x.relay(y)
    out = run_far(panels=first.far, total=total, out=(rows, width), column=0)
    for j, x in enumerate(rest, 1):
        total = run(x.late(), base=totals[j - 1], scale=1.0)
        out = run_far(panels=x.far, total=total, out=out, column=j)
    return out.reshape(rows, 1, width)


def solution(mesh):
    return jax.shard_map(
        shards,
        mesh=mesh,
        in_specs=(P("row", "col"), P(), P()),
        out_specs=P("row", "layer", "col"),
        check_vma=False,
    )
```

time: 311 us -> 298 us (0.958)
  waiting for transfers between devices: 107 us -> 80.1 us
  Pallas kernels: 160 us -> 166 us
  local copies, waits for them, and re-layouts: 19.9 us -> 23.8 us
    ppermute x21, waiting for transfers between devices: 107 us -> 80.1 us  [swap(): return lax.ppermute(x, axis, [(i, i ^ distance) for i in range(size)])]
    pallas_call x7 -> x8, Pallas kernels: 150 us -> 157 us  [the longest x5 118 us: product(): pl.pallas_call(functools.partial(product_kernel, plan, full, scale), grid...]
    slice x4, local copies, waits for them, and re-layouts: 5.81 us -> 9.17 us  [__init__(): self.hops = (self.across[0][:half], self.along[0][half:])]
  transfers between devices with their start and end apart: 21 -> 21, of which waited for: 11 -> 5; matrix products, arithmetic and copies ran while one was open for 6% -> 8% of each run, Pallas kernels for 47% -> 52%
where the time goes in v3:
time: 298 us; the launch traced here: 296 us
  Pallas kernels  166 us (56%)
  waiting for transfers between devices  80.1 us (27%)
  starting transfers between devices  24.3 us (8%)
  local copies, waits for them, and re-layouts  23.8 us (8%)
    pallas_call x5, Pallas kernels, product(): pl.pallas_call(functools.partial(product_kernel, plan, full, scale), grid...  118 us
    ppermute x21, waiting for transfers between devices, swap(): return lax.ppermute(x, axis, [(i, i ^ distance) for i in range(size)])  80.1 us
    pallas_call x3, Pallas kernels, far_product(): pl.pallas_call(functools.partial(far_kernel, column), grid_spec=pltpu.Pre...  38.7 us
    ppermute x21, starting transfers between devices, swap(): return lax.ppermute(x, axis, [(i, i ^ distance) for i in range(size)])  24.3 us
    pallas_call x2, Pallas kernels, pick_columns(): pl.pallas_call(functools.partial(pick_kernel, start), grid_spec=pltpu.Pre...  9.69 us
    slice x4, local copies, waits for them, and re-layouts, __init__(): self.hops = (self.across[0][:half], self.along[0][half:])  9.17 us
    slice x2, local copies, waits for them, and re-layouts, __init__(): self.top, self.bottom = (own[:half], own[half:])  5.98 us
  transfers between devices with their start and end apart: 21, of which 5 were waited for; matrix products, arithmetic and copies ran while one was open for 8% of the time, Pallas kernels for 52%

profile of v3, /device:TPU:0, one launch (start us, length us, event | category | flops | bytes accessed | tf_op | source)
XLA Modules:
  0.0 296.1 jit_solution(14358213631200093173)
XLA Ops:
  2.0 4.8 %pick_columns.3.refs_8_ = bf16[2048,512]{1,0:T(8,128)(2,1)} custom-call(s32[1]{0:T(128)} %bitcast.17.where, s32[16,8]{1,0:T(8,128)} %copy.12.keep, bf16[2048,4096]{1,0:T(8,128)(2,1)} %first_ref.5, bf16[2048,4096]{1,0:T(8,128)(2,1)} %first_ref.5, bf16[2048,4096]{1,0:T(8,128)(2,1)} %first_ref.5, bf16[2048,4096]{1,0:T(8,128)(2,1)} %first_ref.5), custom_call_target="tpu_custom_call" | custom-call | tf_op jit(solution)/shard_map/pick_columns/pallas_call | solution.py:75
  6.8 2.5 collective-permute-start.2
  10.8 4.9 %pick_columns.2.refs_8_ = bf16[2048,512]{1,0:T(8,128)(2,1)} custom-call(s32[1]{0:T(128)} %bitcast.17.where, s32[16,8]{1,0:T(8,128)} %copy.12.keep, bf16[2048,4096]{1,0:T(8,128)(2,1)} %first_ref.5, bf16[2048,4096]{1,0:T(8,128)(2,1)} %first_ref.5, bf16[2048,4096]{1,0:T(8,128)(2,1)} %first_ref.5, bf16[2048,4096]{1,0:T(8,128)(2,1)} %first_ref.5), custom_call_target="tpu_custom_call" | custom-call | tf_op jit(solution)/shard_map/pick_columns/pallas_call | solution.py:75
  15.7 3.0 %fusion.1 = (bf16[1024,512]{1,0:T(8,128)(2,1)}, bf16[1024,512]{1,0:T(8,128)(2,1)}) fusion(bf16[2048,512]{1,0:T(8,128)(2,1)} %pick_columns.2.refs_8_), kind=kLoop, calls=%fused_computation.5 | loop fusion | bytes 4194304 | tf_op jit(solution)/shard_map/slice | solution.py:30
  21.9 34.2 %collective-permute-done.2.refs_9_ = bf16[2048,512]{1,0:T(8,128)(2,1)} collective-permute-done((bf16[2048,512]{1,0:T(8,128)(2,1)}, bf16[2048,512]{1,0:T(8,128)(2,1)}, u32[]{:S(2)}, u32[]{:S(2)}) %collective-permute-start.2) | collective-permute-done | bytes 2097184 | tf_op jit(solution)/shard_map/ppermute | solution.py:17
  56.1 2.3 slice.34
  58.4 2.4 slice.35
  60.8 2.0 collective-permute-start.13
  64.2 25.2 %product.5.total_in = f32[2048,512]{1,0:T(8,128)} custom-call(s32[16]{0:T(128)} %stack.198.meta, bf16[2048,4096]{1,0:T(8,128)(2,1)} %first_ref.5, bf16[2048,4096]{1,0:T(8,128)(2,1)} %first_ref.5, bf16[2048,4096]{1,0:T(8,128)(2,1)} %collective-permute-done.refs_2_.refs_3_.second_ref, bf16[2048,4096]{1,0:T(8,128)(2,1)} %collective-permute-done.refs_2_.refs_3_.second_ref, ...), custom_call_target="tpu_custom_call" | custom-call | flops 12884901888 | bytes 25165824 | tf_op jit(solution)/shard_map/product/pallas_call | solution.py:265
  92.1 11.0 %collective-permute-done.13.top = bf16[1024,512]{1,0:T(8,128)(2,1)} collective-permute-done((bf16[1024,512]{1,0:T(8,128)(2,1)}, bf16[1024,512]{1,0:T(8,128)(2,1)}, u32[]{:S(2)}, u32[]{:S(2)}) %collective-permute-start.13) | collective-permute-done | bytes 1048608 | tf_op jit(solution)/shard_map/ppermute | solution.py:17
  105.2 13.4 %far_product.3 = (f32[2048,512]{1,0:T(8,128)}, bf16[2048,512]{1,0:T(8,128)(2,1)}) custom-call(s32[3]{0:T(128)} %pad_add_fusion.meta, s32[16,8]{1,0:T(8,128)} %copy.16.keep, bf16[2048,4096]{1,0:T(8,128)(2,1)} %first_ref.5, bf16[2048,4096]{1,0:T(8,128)(2,1)} %collective-permute-done.refs_2_.refs_3_.second_ref, ...), custom_call_target="tpu_custom_call" | custom-call | flops 4294967296 | bytes 8388608 | tf_op jit(solution)/shard_map/far_product/pallas_call | solution.py:206
  118.6 2.1 collective-permute-start.15
  120.7 2.9 collective-permute-done.8.refs_14_
  126.8 21.2 %collective-permute-done.5.refs_11_ = bf16[1024,512]{1,0:T(8,128)(2,1)} collective-permute-done((bf16[1024,512]{1,0:T(8,128)(2,1)}, bf16[1024,512]{1,0:T(8,128)(2,1)}, u32[]{:S(2)}, u32[]{:S(2)}) %collective-permute-start.5) | collective-permute-done | bytes 1048608 | tf_op jit(solution)/shard_map/ppermute | solution.py:17
  148.0 27.0 %product.6 = (f32[2048,512]{1,0:T(8,128)}, bf16[2048,512]{1,0:T(8,128)(2,1)}) custom-call(s32[16]{0:T(128)} %stack.96.meta, bf16[2048,4096]{1,0:T(8,128)(2,1)} %first_ref.5, bf16[2048,4096]{1,0:T(8,128)(2,1)} %first_ref.5, bf16[2048,4096]{1,0:T(8,128)(2,1)} %collective-permute-done.refs_2_.refs_3_.second_ref, ...), custom_call_target="tpu_custom_call" | custom-call | flops 17179869184 | bytes 33554432 | tf_op jit(solution)/shard_map/product/pallas_call | solution.py:265
  175.0 3.0 %fusion = (bf16[1024,512]{1,0:T(8,128)(2,1)}, bf16[1024,512]{1,0:T(8,128)(2,1)}) fusion(bf16[2048,512]{1,0:T(8,128)(2,1)} %get-tuple-element.26.refs_8_), kind=kLoop, calls=%fused_computation.4 | loop fusion | bytes 4194304 | tf_op jit(solution)/shard_map/slice | solution.py:30
  180.1 10.9 %collective-permute-done.15.refs_9_ = bf16[2048,512]{1,0:T(8,128)(2,1)} collective-permute-done((bf16[2048,512]{1,0:T(8,128)(2,1)}, bf16[2048,512]{1,0:T(8,128)(2,1)}, u32[]{:S(2)}, u32[]{:S(2)}) %collective-permute-start.15) | collective-permute-done | bytes 2097184 | tf_op jit(solution)/shard_map/ppermute | solution.py:17
  190.9 2.3 slice.36
  195.2 2.3 slice.37
  198.9 25.9 %product.8.total_in = f32[2048,512]{1,0:T(8,128)} custom-call(s32[16]{0:T(128)} %stack.198.meta, bf16[2048,4096]{1,0:T(8,128)(2,1)} %first_ref.5, bf16[2048,4096]{1,0:T(8,128)(2,1)} %first_ref.5, bf16[2048,4096]{1,0:T(8,128)(2,1)} %collective-permute-done.refs_2_.refs_3_.second_ref, bf16[2048,4096]{1,0:T(8,128)(2,1)} %collective-permute-done.refs_2_.refs_3_.second_ref, ...), custom_call_target="tpu_custom_call" | custom-call | flops 12884901888 | bytes 25165824 | tf_op jit(solution)/shard_map/product/pallas_call | solution.py:265
  226.4 22.8 %product.7.refs_10_ = f32[2048,512]{1,0:T(8,128)} custom-call(s32[16]{0:T(128)} %stack.207.meta, bf16[2048,4096]{1,0:T(8,128)(2,1)} %first_ref.5, bf16[2048,4096]{1,0:T(8,128)(2,1)} %first_ref.5, bf16[2048,4096]{1,0:T(8,128)(2,1)} %collective-permute-done.refs_2_.refs_3_.second_ref, bf16[2048,4096]{1,0:T(8,128)(2,1)} %collective-permute-done.refs_2_.refs_3_.second_ref, ...), custom_call_target="tpu_custom_call" | custom-call | flops 8589934592 | bytes 16777216 | tf_op jit(solution)/shard_map/product/pallas_call | solution.py:265
  252.6 12.7 %far_product.4.outs_0_ = bf16[2048,1024]{1,0:T(8,128)(2,1)} custom-call(s32[3]{0:T(128)} %pad_add_fusion.meta, s32[16,8]{1,0:T(8,128)} %copy.16.keep, bf16[2048,4096]{1,0:T(8,128)(2,1)} %first_ref.5, bf16[2048,4096]{1,0:T(8,128)(2,1)} %collective-permute-done.refs_2_.refs_3_.second_ref, f32[8,2,8192]{2,1,0:T(2,128)} %reshape_reshape.3.refs_4_.refs_5_.refs_6_.refs_7_.mask, ...), custom_call_target="tpu_custom_call" | custom-call | flops 4294967296 | bytes 8388608 | tf_op jit(solution)/shard_map/far_product/pallas_call | solution.py:206
  265.3 17.1 %product.9.total_in = f32[2048,512]{1,0:T(8,128)} custom-call(s32[16]{0:T(128)} %stack.216.meta, bf16[2048,4096]{1,0:T(8,128)(2,1)} %first_ref.5, bf16[2048,4096]{1,0:T(8,128)(2,1)} %first_ref.5, bf16[2048,4096]{1,0:T(8,128)(2,1)} %collective-permute-done.refs_2_.refs_3_.second_ref, bf16[2048,4096]{1,0:T(8,128)(2,1)} %collective-permute-done.refs_2_.refs_3_.second_ref, ...), custom_call_target="tpu_custom_call" | custom-call | flops 4294967296 | bytes 8388608 | tf_op jit(solution)/shard_map/product/pallas_call | solution.py:265
  283.4 12.7 %far_product.5 = bf16[2048,1024]{1,0:T(8,128)(2,1)} custom-call(s32[3]{0:T(128)} %pad_add_fusion.meta, s32[16,8]{1,0:T(8,128)} %copy.16.keep, bf16[2048,4096]{1,0:T(8,128)(2,1)} %first_ref.5, bf16[2048,4096]{1,0:T(8,128)(2,1)} %collective-permute-done.refs_2_.refs_3_.second_ref, ...), custom_call_target="tpu_custom_call", output_to_operand_aliasing={{}: (8, {})} | custom-call | flops 4294967296 | bytes 8388608 | tf_op jit(solution)/shard_map/far_product/pallas_call | solution.py:206
  (56 shorter events, 27.7 us)
Async XLA Ops:
  0.0 60.8 %collective-permute-start = (bf16[2048,4096]{1,0:T(8,128)(2,1)}, bf16[2048,4096]{1,0:T(8,128)(2,1)}, u32[]{:S(2)}, u32[]{:S(2)}) collective-permute-start(bf16[2048,4096]{1,0:T(8,128)(2,1)} %first_ref.5), channel_id=1, source_target_pairs={{0,4},{4,0},{1,5},{5,1},{2,6},{6,2},{3,7},{7,3},{8,12},{12,8},{9,1... | collective-permute-start | bytes 50331656 | tf_op jit(solution)/shard_map/ppermute | solution.py:17
  6.8 49.3 %collective-permute-start.2 = (bf16[2048,512]{1,0:T(8,128)(2,1)}, bf16[2048,512]{1,0:T(8,128)(2,1)}, u32[]{:S(2)}, u32[]{:S(2)}) collective-permute-start(bf16[2048,512]{1,0:T(8,128)(2,1)} %pick_columns.3.refs_8_), channel_id=1, source_target_pairs={{0,8},{8,0},{16,24},{24,16},{1,9},{9,1},{17,25},{25,17},{2,10},{10... | collective-permute-start | bytes 6291464 | tf_op jit(solution)/shard_map/ppermute | solution.py:17
  9.3 49.1 %collective-permute-start.3 = (bf16[2048,512]{1,0:T(8,128)(2,1)}, bf16[2048,512]{1,0:T(8,128)(2,1)}, u32[]{:S(2)}, u32[]{:S(2)}) collective-permute-start(bf16[2048,512]{1,0:T(8,128)(2,1)} %pick_columns.3.refs_8_), channel_id=1, source_target_pairs={{0,16},{8,24},{16,0},{24,8},{1,17},{9,25},{17,1},{25,9},{2,18},{10... | collective-permute-start | bytes 6291464 | tf_op jit(solution)/shard_map/ppermute | solution.py:17
  18.7 70.7 %collective-permute-start.6 = (bf16[1024,512]{1,0:T(8,128)(2,1)}, bf16[1024,512]{1,0:T(8,128)(2,1)S(1)}, u32[]{:S(2)}, u32[]{:S(2)}) collective-permute-start(bf16[1024,512]{1,0:T(8,128)(2,1)} %get-tuple-element.22), channel_id=1, source_target_pairs={{0,16},{8,24},{16,0},{24,8},{1,17},{9,25},{17,1},{25,9},{2,18},{10... | collective-permute-start | bytes 3145736 | tf_op jit(solution)/shard_map/ppermute | solution.py:17
  19.2 70.8 %collective-permute-start.1 = (bf16[1024,512]{1,0:T(8,128)(2,1)}, bf16[1024,512]{1,0:T(8,128)(2,1)}, u32[]{:S(2)}, u32[]{:S(2)}) collective-permute-start(bf16[1024,512]{1,0:T(8,128)(2,1)} %get-tuple-element.23), channel_id=1, source_target_pairs={{0,8},{8,0},{16,24},{24,16},{1,9},{9,1},{17,25},{25,17},{2,10},{10... | collective-permute-start | bytes 3145736 | tf_op jit(solution)/shard_map/ppermute | solution.py:17
  60.8 42.3 %collective-permute-start.13 = (bf16[1024,512]{1,0:T(8,128)(2,1)}, bf16[1024,512]{1,0:T(8,128)(2,1)}, u32[]{:S(2)}, u32[]{:S(2)}) collective-permute-start(bf16[1024,512]{1,0:T(8,128)(2,1)} %slice.34), channel_id=1, source_target_pairs={{0,16},{8,24},{16,0},{24,8},{1,17},{9,25},{17,1},{25,9},{2,18},{10... | collective-permute-start | bytes 3145736 | tf_op jit(solution)/shard_map/ppermute | solution.py:17
  62.7 42.5 %collective-permute-start.14 = (bf16[1024,512]{1,0:T(8,128)(2,1)}, bf16[1024,512]{1,0:T(8,128)(2,1)}, u32[]{:S(2)}, u32[]{:S(2)}) collective-permute-start(bf16[1024,512]{1,0:T(8,128)(2,1)} %slice.35), channel_id=1, source_target_pairs={{0,8},{8,0},{16,24},{24,16},{1,9},{9,1},{17,25},{25,17},{2,10},{10... | collective-permute-start | bytes 3145736 | tf_op jit(solution)/shard_map/ppermute | solution.py:17
  89.4 29.2 %copy-start = (bf16[1024,512]{1,0:T(8,128)(2,1)}, bf16[1024,512]{1,0:T(8,128)(2,1)S(1)}, u32[]{:S(2)}) copy-start(bf16[1024,512]{1,0:T(8,128)(2,1)S(1)} %collective-permute-done.6.refs_12_) | copy-start | bytes 3145732
  89.4 34.1 %collective-permute-start.8 = (bf16[1024,512]{1,0:T(8,128)(2,1)S(1)}, bf16[1024,512]{1,0:T(8,128)(2,1)}, u32[]{:S(2)}, u32[]{:S(2)}) collective-permute-start(bf16[1024,512]{1,0:T(8,128)(2,1)S(1)} %collective-permute-done.6.refs_12_), channel_id=1, source_target_pairs={{0,8},{8,0},{16,24},{24,16},{1,9},{9,1},{17,25},{25,17},{2,10},{10... | collective-permute-start | bytes 3145736 | tf_op jit(solution)/shard_map/ppermute | solution.py:17
  90.0 36.7 %collective-permute-start.7 = (bf16[1024,512]{1,0:T(8,128)(2,1)}, bf16[1024,512]{1,0:T(8,128)(2,1)}, u32[]{:S(2)}, u32[]{:S(2)}) collective-permute-start(bf16[1024,512]{1,0:T(8,128)(2,1)} %collective-permute-done.1.refs_9_), channel_id=1, source_target_pairs={{0,16},{8,24},{16,0},{24,8},{1,17},{9,25},{17,1},{25,9},{2,18},{10... | collective-permute-start | bytes 3145736 | tf_op jit(solution)/shard_map/ppermute | solution.py:17
  90.3 57.7 %collective-permute-start.5 = (bf16[1024,512]{1,0:T(8,128)(2,1)}, bf16[1024,512]{1,0:T(8,128)(2,1)}, u32[]{:S(2)}, u32[]{:S(2)}) collective-permute-start(bf16[1024,512]{1,0:T(8,128)(2,1)} %get-tuple-element.23), channel_id=1, source_target_pairs={{0,16},{8,24},{16,0},{24,8},{1,17},{9,25},{17,1},{25,9},{2,18},{10... | collective-permute-start | bytes 3145736 | tf_op jit(solution)/shard_map/ppermute | solution.py:17
  103.0 44.9 %collective-permute-start.4 = (bf16[1024,512]{1,0:T(8,128)(2,1)}, bf16[1024,512]{1,0:T(8,128)(2,1)}, u32[]{:S(2)}, u32[]{:S(2)}) collective-permute-start(bf16[1024,512]{1,0:T(8,128)(2,1)} %get-tuple-element.22), channel_id=1, source_target_pairs={{0,8},{8,0},{16,24},{24,16},{1,9},{9,1},{17,25},{25,17},{2,10},{10... | collective-permute-start | bytes 3145736 | tf_op jit(solution)/shard_map/ppermute | solution.py:17
  118.6 72.3 %collective-permute-start.15 = (bf16[2048,512]{1,0:T(8,128)(2,1)}, bf16[2048,512]{1,0:T(8,128)(2,1)}, u32[]{:S(2)}, u32[]{:S(2)}) collective-permute-start(bf16[2048,512]{1,0:T(8,128)(2,1)} %get-tuple-element.33.refs_8_), channel_id=1, source_target_pairs={{0,8},{8,0},{16,24},{24,16},{1,9},{9,1},{17,25},{25,17},{2,10},{10... | collective-permute-start | bytes 6291464 | tf_op jit(solution)/shard_map/ppermute | solution.py:17
  123.5 71.7 %collective-permute-start.16 = (bf16[2048,512]{1,0:T(8,128)(2,1)}, bf16[2048,512]{1,0:T(8,128)(2,1)}, u32[]{:S(2)}, u32[]{:S(2)}) collective-permute-start(bf16[2048,512]{1,0:T(8,128)(2,1)} %get-tuple-element.33.refs_8_), channel_id=1, source_target_pairs={{0,16},{8,24},{16,0},{24,8},{1,17},{9,25},{17,1},{25,9},{2,18},{10... | collective-permute-start | bytes 6291464 | tf_op jit(solution)/shard_map/ppermute | solution.py:17
  178.0 47.4 %collective-permute-start.10 = (bf16[1024,512]{1,0:T(8,128)(2,1)}, bf16[1024,512]{1,0:T(8,128)(2,1)S(1)}, u32[]{:S(2)}, u32[]{:S(2)}) collective-permute-start(bf16[1024,512]{1,0:T(8,128)(2,1)} %get-tuple-element.35), channel_id=1, source_target_pairs={{0,16},{8,24},{16,0},{24,8},{1,17},{9,25},{17,1},{25,9},{2,18},{10... | collective-permute-start | bytes 3145736 | tf_op jit(solution)/shard_map/ppermute | solution.py:17
  179.5 46.2 %collective-permute-start.9 = (bf16[1024,512]{1,0:T(8,128)(2,1)}, bf16[1024,512]{1,0:T(8,128)(2,1)}, u32[]{:S(2)}, u32[]{:S(2)}) collective-permute-start(bf16[1024,512]{1,0:T(8,128)(2,1)} %get-tuple-element.36), channel_id=1, source_target_pairs={{0,8},{8,0},{16,24},{24,16},{1,9},{9,1},{17,25},{25,17},{2,10},{10... | collective-permute-start | bytes 3145736 | tf_op jit(solution)/shard_map/ppermute | solution.py:17
  193.2 57.2 %collective-permute-start.19 = (bf16[1024,512]{1,0:T(8,128)(2,1)}, bf16[1024,512]{1,0:T(8,128)(2,1)}, u32[]{:S(2)}, u32[]{:S(2)}) collective-permute-start(bf16[1024,512]{1,0:T(8,128)(2,1)} %slice.36), channel_id=1, source_target_pairs={{0,16},{8,24},{16,0},{24,8},{1,17},{9,25},{17,1},{25,9},{2,18},{10... | collective-permute-start | bytes 3145736 | tf_op jit(solution)/shard_map/ppermute | solution.py:17
  197.4 55.2 %collective-permute-start.20 = (bf16[1024,512]{1,0:T(8,128)(2,1)}, bf16[1024,512]{1,0:T(8,128)(2,1)}, u32[]{:S(2)}, u32[]{:S(2)}) collective-permute-start(bf16[1024,512]{1,0:T(8,128)(2,1)} %slice.37), channel_id=1, source_target_pairs={{0,8},{8,0},{16,24},{24,16},{1,9},{9,1},{17,25},{25,17},{2,10},{10... | collective-permute-start | bytes 3145736 | tf_op jit(solution)/shard_map/ppermute | solution.py:17
  224.8 40.5 %collective-permute-start.18 = (bf16[1024,512]{1,0:T(8,128)(2,1)}, bf16[1024,512]{1,0:T(8,128)(2,1)}, u32[]{:S(2)}, u32[]{:S(2)}) collective-permute-start(bf16[1024,512]{1,0:T(8,128)(2,1)} %get-tuple-element.36), channel_id=1, source_target_pairs={{0,16},{8,24},{16,0},{24,8},{1,17},{9,25},{17,1},{25,9},{2,18},{10... | collective-permute-start | bytes 3145736 | tf_op jit(solution)/shard_map/ppermute | solution.py:17
  225.4 1.0 copy-start.1
  225.4 39.9 %collective-permute-start.17 = (bf16[1024,512]{1,0:T(8,128)(2,1)}, bf16[1024,512]{1,0:T(8,128)(2,1)}, u32[]{:S(2)}, u32[]{:S(2)}) collective-permute-start(bf16[1024,512]{1,0:T(8,128)(2,1)} %get-tuple-element.35), channel_id=1, source_target_pairs={{0,8},{8,0},{16,24},{24,16},{1,9},{9,1},{17,25},{25,17},{2,10},{10... | collective-permute-start | bytes 3145736 | tf_op jit(solution)/shard_map/ppermute | solution.py:17
  249.2 33.2 %collective-permute-start.12 = (bf16[1024,512]{1,0:T(8,128)(2,1)}, bf16[1024,512]{1,0:T(8,128)(2,1)S(1)}, u32[]{:S(2)}, u32[]{:S(2)}) collective-permute-start(bf16[1024,512]{1,0:T(8,128)(2,1)} %copy-done.1), channel_id=1, source_target_pairs={{0,8},{8,0},{16,24},{24,16},{1,9},{9,1},{17,25},{25,17},{2,10},{10... | collective-permute-start | bytes 3145736 | tf_op jit(solution)/shard_map/ppermute | solution.py:17
  250.4 32.1 %collective-permute-start.11 = (bf16[1024,512]{1,0:T(8,128)(2,1)}, bf16[1024,512]{1,0:T(8,128)(2,1)}, u32[]{:S(2)}, u32[]{:S(2)}) collective-permute-start(bf16[1024,512]{1,0:T(8,128)(2,1)} %collective-permute-done.9.refs_9_), channel_id=1, source_target_pairs={{0,16},{8,24},{16,0},{24,8},{1,17},{9,25},{17,1},{25,9},{2,18},{10... | collective-permute-start | bytes 3145736 | tf_op jit(solution)/shard_map/ppermute | solution.py:17
  282.4 1.0 copy-start.2

commit v4 on v3

--- a/solution.py
+++ b/solution.py
@@ -169,7 +169,8 @@
 
 def far_product(slots, owners, keep, sources, mask, panels, total, out=None, column=None):
     rows, width = total.shape
-    tile, depth = TILE * B, rows
+    tile, depth = 2 * TILE * B, rows
+    mask = mask.reshape(rows // tile, 2 * TILE, mask.shape[2])
     n_slot = len(slots)
     per_source = n_slot // len(sources)
     slot = slots[-1]
@@ -188,7 +189,7 @@
     row_block = pl.BlockSpec((tile, width), lambda i, *_: (i, 0))
     specs = [
         rows_of(0), rows_of(1),
-        pl.BlockSpec((1, TILE, depth), lambda i, meta, keep: (i, 0, meta[2])),
+        pl.BlockSpec((1, 2 * TILE, depth), lambda i, meta, keep: (i, 0, meta[2])),
         panel, panel, row_block,
     ]
     args = [*sources, mask, *panels, total]

time: 298 us -> 295 us (0.990)
  Pallas kernels: 166 us -> 163 us
    pallas_call x3, Pallas kernels: 38.7 us -> 35.4 us  [far_product(): pl.pallas_call(functools.partial(far_kernel, column), grid_spec=pltpu.Pre...]
  transfers between devices with their start and end apart: 21 -> 21, of which waited for: 5 -> 6; matrix products, arithmetic and copies ran while one was open for 8% -> 8% of each run, Pallas kernels for 52% -> 52%
where the time goes in v4:
time: 295 us; the launch traced here: 294 us
  Pallas kernels  163 us (55%)
  waiting for transfers between devices  80.9 us (27%)
  starting transfers between devices  24.3 us (8%)
  local copies, waits for them, and re-layouts  23.9 us (8%)
    pallas_call x5, Pallas kernels, product(): pl.pallas_call(functools.partial(product_kernel, plan, full, scale), grid...  118 us
    ppermute x21, waiting for transfers between devices, swap(): return lax.ppermute(x, axis, [(i, i ^ distance) for i in range(size)])  80.9 us
    pallas_call x3, Pallas kernels, far_product(): pl.pallas_call(functools.partial(far_kernel, column), grid_spec=pltpu.Pre...  35.4 us
    ppermute x21, starting transfers between devices, swap(): return lax.ppermute(x, axis, [(i, i ^ distance) for i in range(size)])  24.3 us
    pallas_call x2, Pallas kernels, pick_columns(): pl.pallas_call(functools.partial(pick_kernel, start), grid_spec=pltpu.Pre...  9.69 us
    slice x4, local copies, waits for them, and re-layouts, __init__(): self.hops = (self.across[0][:half], self.along[0][half:])  9.17 us
    slice x2, local copies, waits for them, and re-layouts, __init__(): self.top, self.bottom = (own[:half], own[half:])  5.98 us
  transfers between devices with their start and end apart: 21, of which 6 were waited for; matrix products, arithmetic and copies ran while one was open for 8% of the time, Pallas kernels for 52%

profile of v4, /device:TPU:0, one launch (start us, length us, event | category | flops | bytes accessed | tf_op | source)
XLA Modules:
  0.0 293.6 jit_solution(15394021794893061487)
XLA Ops:
  2.0 4.8 %pick_columns.3.refs_8_ = bf16[2048,512]{1,0:T(8,128)(2,1)} custom-call(s32[1]{0:T(128)} %bitcast.17.where, s32[16,8]{1,0:T(8,128)} %copy.12.keep, bf16[2048,4096]{1,0:T(8,128)(2,1)} %first_ref.5, bf16[2048,4096]{1,0:T(8,128)(2,1)} %first_ref.5, bf16[2048,4096]{1,0:T(8,128)(2,1)} %first_ref.5, bf16[2048,4096]{1,0:T(8,128)(2,1)} %first_ref.5), custom_call_target="tpu_custom_call" | custom-call | tf_op jit(solution)/shard_map/pick_columns/pallas_call | solution.py:75
  6.8 2.5 collective-permute-start.2
  10.8 4.9 %pick_columns.2.refs_8_ = bf16[2048,512]{1,0:T(8,128)(2,1)} custom-call(s32[1]{0:T(128)} %bitcast.17.where, s32[16,8]{1,0:T(8,128)} %copy.12.keep, bf16[2048,4096]{1,0:T(8,128)(2,1)} %first_ref.5, bf16[2048,4096]{1,0:T(8,128)(2,1)} %first_ref.5, bf16[2048,4096]{1,0:T(8,128)(2,1)} %first_ref.5, bf16[2048,4096]{1,0:T(8,128)(2,1)} %first_ref.5), custom_call_target="tpu_custom_call" | custom-call | tf_op jit(solution)/shard_map/pick_columns/pallas_call | solution.py:75
  15.7 3.0 %fusion.1 = (bf16[1024,512]{1,0:T(8,128)(2,1)}, bf16[1024,512]{1,0:T(8,128)(2,1)}) fusion(bf16[2048,512]{1,0:T(8,128)(2,1)} %pick_columns.2.refs_8_), kind=kLoop, calls=%fused_computation.5 | loop fusion | bytes 4194304 | tf_op jit(solution)/shard_map/slice | solution.py:30
  21.9 34.2 %collective-permute-done.2.refs_9_ = bf16[2048,512]{1,0:T(8,128)(2,1)} collective-permute-done((bf16[2048,512]{1,0:T(8,128)(2,1)}, bf16[2048,512]{1,0:T(8,128)(2,1)}, u32[]{:S(2)}, u32[]{:S(2)}) %collective-permute-start.2) | collective-permute-done | bytes 2097184 | tf_op jit(solution)/shard_map/ppermute | solution.py:17
  56.1 2.3 slice.34
  58.4 2.4 slice.35
  60.8 2.0 collective-permute-start.13
  64.2 25.2 %product.5.total_in = f32[2048,512]{1,0:T(8,128)} custom-call(s32[16]{0:T(128)} %stack.198.meta, bf16[2048,4096]{1,0:T(8,128)(2,1)} %first_ref.5, bf16[2048,4096]{1,0:T(8,128)(2,1)} %first_ref.5, bf16[2048,4096]{1,0:T(8,128)(2,1)} %collective-permute-done.refs_2_.refs_3_.second_ref, bf16[2048,4096]{1,0:T(8,128)(2,1)} %collective-permute-done.refs_2_.refs_3_.second_ref, ...), custom_call_target="tpu_custom_call" | custom-call | flops 12884901888 | bytes 25165824 | tf_op jit(solution)/shard_map/product/pallas_call | solution.py:266
  92.1 11.0 %collective-permute-done.13.top = bf16[1024,512]{1,0:T(8,128)(2,1)} collective-permute-done((bf16[1024,512]{1,0:T(8,128)(2,1)}, bf16[1024,512]{1,0:T(8,128)(2,1)}, u32[]{:S(2)}, u32[]{:S(2)}) %collective-permute-start.13) | collective-permute-done | bytes 1048608 | tf_op jit(solution)/shard_map/ppermute | solution.py:17
  106.3 12.5 %far_product.3 = (f32[2048,512]{1,0:T(8,128)}, bf16[2048,512]{1,0:T(8,128)(2,1)}) custom-call(s32[3]{0:T(128)} %pad_add_fusion.meta, s32[16,8]{1,0:T(8,128)} %copy.16.keep, bf16[2048,4096]{1,0:T(8,128)(2,1)} %first_ref.5, bf16[2048,4096]{1,0:T(8,128)(2,1)} %collective-permute-done.refs_2_.refs_3_.second_ref, f32[4,4,8192]{2,1,0:T(4,128)} %reshape_reshape_reshape.2.mask, ...), custom_call_target="tpu_custom_call" | custom-call | flops 4294967296 | bytes 8388608 | tf_op jit(solution)/shard_map/far_product/pallas_call | solution.py:207
  118.8 2.0 collective-permute-start.15
  120.8 2.7 collective-permute-done.8.refs_14_
  126.8 21.2 %collective-permute-done.5.refs_11_ = bf16[1024,512]{1,0:T(8,128)(2,1)} collective-permute-done((bf16[1024,512]{1,0:T(8,128)(2,1)}, bf16[1024,512]{1,0:T(8,128)(2,1)}, u32[]{:S(2)}, u32[]{:S(2)}) %collective-permute-start.5) | collective-permute-done | bytes 1048608 | tf_op jit(solution)/shard_map/ppermute | solution.py:17
  148.0 27.0 %product.6 = (f32[2048,512]{1,0:T(8,128)}, bf16[2048,512]{1,0:T(8,128)(2,1)}) custom-call(s32[16]{0:T(128)} %stack.96.meta, bf16[2048,4096]{1,0:T(8,128)(2,1)} %first_ref.5, bf16[2048,4096]{1,0:T(8,128)(2,1)} %first_ref.5, bf16[2048,4096]{1,0:T(8,128)(2,1)} %collective-permute-done.refs_2_.refs_3_.second_ref, ...), custom_call_target="tpu_custom_call" | custom-call | flops 17179869184 | bytes 33554432 | tf_op jit(solution)/shard_map/product/pallas_call | solution.py:266
  175.0 3.0 %fusion = (bf16[1024,512]{1,0:T(8,128)(2,1)}, bf16[1024,512]{1,0:T(8,128)(2,1)}) fusion(bf16[2048,512]{1,0:T(8,128)(2,1)} %get-tuple-element.26.refs_8_), kind=kLoop, calls=%fused_computation.4 | loop fusion | bytes 4194304 | tf_op jit(solution)/shard_map/slice | solution.py:30
  180.1 10.9 %collective-permute-done.15.refs_9_ = bf16[2048,512]{1,0:T(8,128)(2,1)} collective-permute-done((bf16[2048,512]{1,0:T(8,128)(2,1)}, bf16[2048,512]{1,0:T(8,128)(2,1)}, u32[]{:S(2)}, u32[]{:S(2)}) %collective-permute-start.15) | collective-permute-done | bytes 2097184 | tf_op jit(solution)/shard_map/ppermute | solution.py:17
  190.9 2.3 slice.36
  195.2 2.3 slice.37
  198.9 25.9 %product.8.total_in = f32[2048,512]{1,0:T(8,128)} custom-call(s32[16]{0:T(128)} %stack.198.meta, bf16[2048,4096]{1,0:T(8,128)(2,1)} %first_ref.5, bf16[2048,4096]{1,0:T(8,128)(2,1)} %first_ref.5, bf16[2048,4096]{1,0:T(8,128)(2,1)} %collective-permute-done.refs_2_.refs_3_.second_ref, bf16[2048,4096]{1,0:T(8,128)(2,1)} %collective-permute-done.refs_2_.refs_3_.second_ref, ...), custom_call_target="tpu_custom_call" | custom-call | flops 12884901888 | bytes 25165824 | tf_op jit(solution)/shard_map/product/pallas_call | solution.py:266
  226.4 22.8 %product.7.refs_10_ = f32[2048,512]{1,0:T(8,128)} custom-call(s32[16]{0:T(128)} %stack.207.meta, bf16[2048,4096]{1,0:T(8,128)(2,1)} %first_ref.5, bf16[2048,4096]{1,0:T(8,128)(2,1)} %first_ref.5, bf16[2048,4096]{1,0:T(8,128)(2,1)} %collective-permute-done.refs_2_.refs_3_.second_ref, bf16[2048,4096]{1,0:T(8,128)(2,1)} %collective-permute-done.refs_2_.refs_3_.second_ref, ...), custom_call_target="tpu_custom_call" | custom-call | flops 8589934592 | bytes 16777216 | tf_op jit(solution)/shard_map/product/pallas_call | solution.py:266
  252.6 11.5 %far_product.4.outs_0_ = bf16[2048,1024]{1,0:T(8,128)(2,1)} custom-call(s32[3]{0:T(128)} %pad_add_fusion.meta, s32[16,8]{1,0:T(8,128)} %copy.16.keep, bf16[2048,4096]{1,0:T(8,128)(2,1)} %first_ref.5, bf16[2048,4096]{1,0:T(8,128)(2,1)} %collective-permute-done.refs_2_.refs_3_.second_ref, f32[4,4,8192]{2,1,0:T(4,128)} %reshape_reshape_reshape.2.mask, ...), custom_call_target="tpu_custom_call" | custom-call | flops 4294967296 | bytes 8388608 | tf_op jit(solution)/shard_map/far_product/pallas_call | solution.py:207
  264.1 17.1 %product.9.total_in = f32[2048,512]{1,0:T(8,128)} custom-call(s32[16]{0:T(128)} %stack.216.meta, bf16[2048,4096]{1,0:T(8,128)(2,1)} %first_ref.5, bf16[2048,4096]{1,0:T(8,128)(2,1)} %first_ref.5, bf16[2048,4096]{1,0:T(8,128)(2,1)} %collective-permute-done.refs_2_.refs_3_.second_ref, bf16[2048,4096]{1,0:T(8,128)(2,1)} %collective-permute-done.refs_2_.refs_3_.second_ref, ...), custom_call_target="tpu_custom_call" | custom-call | flops 4294967296 | bytes 8388608 | tf_op jit(solution)/shard_map/product/pallas_call | solution.py:266
  282.2 11.5 %far_product.5 = bf16[2048,1024]{1,0:T(8,128)(2,1)} custom-call(s32[3]{0:T(128)} %pad_add_fusion.meta, s32[16,8]{1,0:T(8,128)} %copy.16.keep, bf16[2048,4096]{1,0:T(8,128)(2,1)} %first_ref.5, bf16[2048,4096]{1,0:T(8,128)(2,1)} %collective-permute-done.refs_2_.refs_3_.second_ref, ...), custom_call_target="tpu_custom_call", output_to_operand_aliasing={{}: (8, {})} | custom-call | flops 4294967296 | bytes 8388608 | tf_op jit(solution)/shard_map/far_product/pallas_call | solution.py:207
  (57 shorter events, 28.8 us)
Async XLA Ops:
  0.0 60.8 %collective-permute-start = (bf16[2048,4096]{1,0:T(8,128)(2,1)}, bf16[2048,4096]{1,0:T(8,128)(2,1)}, u32[]{:S(2)}, u32[]{:S(2)}) collective-permute-start(bf16[2048,4096]{1,0:T(8,128)(2,1)} %first_ref.5), channel_id=1, source_target_pairs={{0,4},{4,0},{1,5},{5,1},{2,6},{6,2},{3,7},{7,3},{8,12},{12,8},{9,1... | collective-permute-start | bytes 50331656 | tf_op jit(solution)/shard_map/ppermute | solution.py:17
  6.8 49.3 %collective-permute-start.2 = (bf16[2048,512]{1,0:T(8,128)(2,1)}, bf16[2048,512]{1,0:T(8,128)(2,1)}, u32[]{:S(2)}, u32[]{:S(2)}) collective-permute-start(bf16[2048,512]{1,0:T(8,128)(2,1)} %pick_columns.3.refs_8_), channel_id=1, source_target_pairs={{0,8},{8,0},{16,24},{24,16},{1,9},{9,1},{17,25},{25,17},{2,10},{10... | collective-permute-start | bytes 6291464 | tf_op jit(solution)/shard_map/ppermute | solution.py:17
  9.3 49.1 %collective-permute-start.3 = (bf16[2048,512]{1,0:T(8,128)(2,1)}, bf16[2048,512]{1,0:T(8,128)(2,1)}, u32[]{:S(2)}, u32[]{:S(2)}) collective-permute-start(bf16[2048,512]{1,0:T(8,128)(2,1)} %pick_columns.3.refs_8_), channel_id=1, source_target_pairs={{0,16},{8,24},{16,0},{24,8},{1,17},{9,25},{17,1},{25,9},{2,18},{10... | collective-permute-start | bytes 6291464 | tf_op jit(solution)/shard_map/ppermute | solution.py:17
  18.7 70.7 %collective-permute-start.6 = (bf16[1024,512]{1,0:T(8,128)(2,1)}, bf16[1024,512]{1,0:T(8,128)(2,1)S(1)}, u32[]{:S(2)}, u32[]{:S(2)}) collective-permute-start(bf16[1024,512]{1,0:T(8,128)(2,1)} %get-tuple-element.22), channel_id=1, source_target_pairs={{0,16},{8,24},{16,0},{24,8},{1,17},{9,25},{17,1},{25,9},{2,18},{10... | collective-permute-start | bytes 3145736 | tf_op jit(solution)/shard_map/ppermute | solution.py:17
  19.2 70.8 %collective-permute-start.1 = (bf16[1024,512]{1,0:T(8,128)(2,1)}, bf16[1024,512]{1,0:T(8,128)(2,1)}, u32[]{:S(2)}, u32[]{:S(2)}) collective-permute-start(bf16[1024,512]{1,0:T(8,128)(2,1)} %get-tuple-element.23), channel_id=1, source_target_pairs={{0,8},{8,0},{16,24},{24,16},{1,9},{9,1},{17,25},{25,17},{2,10},{10... | collective-permute-start | bytes 3145736 | tf_op jit(solution)/shard_map/ppermute | solution.py:17
  60.8 42.3 %collective-permute-start.13 = (bf16[1024,512]{1,0:T(8,128)(2,1)}, bf16[1024,512]{1,0:T(8,128)(2,1)}, u32[]{:S(2)}, u32[]{:S(2)}) collective-permute-start(bf16[1024,512]{1,0:T(8,128)(2,1)} %slice.34), channel_id=1, source_target_pairs={{0,16},{8,24},{16,0},{24,8},{1,17},{9,25},{17,1},{25,9},{2,18},{10... | collective-permute-start | bytes 3145736 | tf_op jit(solution)/shard_map/ppermute | solution.py:17
  62.7 43.5 %collective-permute-start.14 = (bf16[1024,512]{1,0:T(8,128)(2,1)}, bf16[1024,512]{1,0:T(8,128)(2,1)}, u32[]{:S(2)}, u32[]{:S(2)}) collective-permute-start(bf16[1024,512]{1,0:T(8,128)(2,1)} %slice.35), channel_id=1, source_target_pairs={{0,8},{8,0},{16,24},{24,16},{1,9},{9,1},{17,25},{25,17},{2,10},{10... | collective-permute-start | bytes 3145736 | tf_op jit(solution)/shard_map/ppermute | solution.py:17
  89.4 29.3 %copy-start = (bf16[1024,512]{1,0:T(8,128)(2,1)}, bf16[1024,512]{1,0:T(8,128)(2,1)S(1)}, u32[]{:S(2)}) copy-start(bf16[1024,512]{1,0:T(8,128)(2,1)S(1)} %collective-permute-done.6.refs_12_) | copy-start | bytes 3145732
  89.4 34.1 %collective-permute-start.8 = (bf16[1024,512]{1,0:T(8,128)(2,1)S(1)}, bf16[1024,512]{1,0:T(8,128)(2,1)}, u32[]{:S(2)}, u32[]{:S(2)}) collective-permute-start(bf16[1024,512]{1,0:T(8,128)(2,1)S(1)} %collective-permute-done.6.refs_12_), channel_id=1, source_target_pairs={{0,8},{8,0},{16,24},{24,16},{1,9},{9,1},{17,25},{25,17},{2,10},{10... | collective-permute-start | bytes 3145736 | tf_op jit(solution)/shard_map/ppermute | solution.py:17
  90.0 36.8 %collective-permute-start.7 = (bf16[1024,512]{1,0:T(8,128)(2,1)}, bf16[1024,512]{1,0:T(8,128)(2,1)}, u32[]{:S(2)}, u32[]{:S(2)}) collective-permute-start(bf16[1024,512]{1,0:T(8,128)(2,1)} %collective-permute-done.1.refs_9_), channel_id=1, source_target_pairs={{0,16},{8,24},{16,0},{24,8},{1,17},{9,25},{17,1},{25,9},{2,18},{10... | collective-permute-start | bytes 3145736 | tf_op jit(solution)/shard_map/ppermute | solution.py:17
  90.3 57.7 %collective-permute-start.5 = (bf16[1024,512]{1,0:T(8,128)(2,1)}, bf16[1024,512]{1,0:T(8,128)(2,1)}, u32[]{:S(2)}, u32[]{:S(2)}) collective-permute-start(bf16[1024,512]{1,0:T(8,128)(2,1)} %get-tuple-element.23), channel_id=1, source_target_pairs={{0,16},{8,24},{16,0},{24,8},{1,17},{9,25},{17,1},{25,9},{2,18},{10... | collective-permute-start | bytes 3145736 | tf_op jit(solution)/shard_map/ppermute | solution.py:17
  103.0 44.9 %collective-permute-start.4 = (bf16[1024,512]{1,0:T(8,128)(2,1)}, bf16[1024,512]{1,0:T(8,128)(2,1)}, u32[]{:S(2)}, u32[]{:S(2)}) collective-permute-start(bf16[1024,512]{1,0:T(8,128)(2,1)} %get-tuple-element.22), channel_id=1, source_target_pairs={{0,8},{8,0},{16,24},{24,16},{1,9},{9,1},{17,25},{25,17},{2,10},{10... | collective-permute-start | bytes 3145736 | tf_op jit(solution)/shard_map/ppermute | solution.py:17
  118.8 72.2 %collective-permute-start.15 = (bf16[2048,512]{1,0:T(8,128)(2,1)}, bf16[2048,512]{1,0:T(8,128)(2,1)}, u32[]{:S(2)}, u32[]{:S(2)}) collective-permute-start(bf16[2048,512]{1,0:T(8,128)(2,1)} %get-tuple-element.33.refs_8_), channel_id=1, source_target_pairs={{0,8},{8,0},{16,24},{24,16},{1,9},{9,1},{17,25},{25,17},{2,10},{10... | collective-permute-start | bytes 6291464 | tf_op jit(solution)/shard_map/ppermute | solution.py:17
  123.5 71.7 %collective-permute-start.16 = (bf16[2048,512]{1,0:T(8,128)(2,1)}, bf16[2048,512]{1,0:T(8,128)(2,1)}, u32[]{:S(2)}, u32[]{:S(2)}) collective-permute-start(bf16[2048,512]{1,0:T(8,128)(2,1)} %get-tuple-element.33.refs_8_), channel_id=1, source_target_pairs={{0,16},{8,24},{16,0},{24,8},{1,17},{9,25},{17,1},{25,9},{2,18},{10... | collective-permute-start | bytes 6291464 | tf_op jit(solution)/shard_map/ppermute | solution.py:17
  178.0 47.4 %collective-permute-start.10 = (bf16[1024,512]{1,0:T(8,128)(2,1)}, bf16[1024,512]{1,0:T(8,128)(2,1)S(1)}, u32[]{:S(2)}, u32[]{:S(2)}) collective-permute-start(bf16[1024,512]{1,0:T(8,128)(2,1)} %get-tuple-element.35), channel_id=1, source_target_pairs={{0,16},{8,24},{16,0},{24,8},{1,17},{9,25},{17,1},{25,9},{2,18},{10... | collective-permute-start | bytes 3145736 | tf_op jit(solution)/shard_map/ppermute | solution.py:17
  179.5 46.2 %collective-permute-start.9 = (bf16[1024,512]{1,0:T(8,128)(2,1)}, bf16[1024,512]{1,0:T(8,128)(2,1)}, u32[]{:S(2)}, u32[]{:S(2)}) collective-permute-start(bf16[1024,512]{1,0:T(8,128)(2,1)} %get-tuple-element.36), channel_id=1, source_target_pairs={{0,8},{8,0},{16,24},{24,16},{1,9},{9,1},{17,25},{25,17},{2,10},{10... | collective-permute-start | bytes 3145736 | tf_op jit(solution)/shard_map/ppermute | solution.py:17
  193.2 57.2 %collective-permute-start.19 = (bf16[1024,512]{1,0:T(8,128)(2,1)}, bf16[1024,512]{1,0:T(8,128)(2,1)}, u32[]{:S(2)}, u32[]{:S(2)}) collective-permute-start(bf16[1024,512]{1,0:T(8,128)(2,1)} %slice.36), channel_id=1, source_target_pairs={{0,16},{8,24},{16,0},{24,8},{1,17},{9,25},{17,1},{25,9},{2,18},{10... | collective-permute-start | bytes 3145736 | tf_op jit(solution)/shard_map/ppermute | solution.py:17
  197.4 55.2 %collective-permute-start.20 = (bf16[1024,512]{1,0:T(8,128)(2,1)}, bf16[1024,512]{1,0:T(8,128)(2,1)}, u32[]{:S(2)}, u32[]{:S(2)}) collective-permute-start(bf16[1024,512]{1,0:T(8,128)(2,1)} %slice.37), channel_id=1, source_target_pairs={{0,8},{8,0},{16,24},{24,16},{1,9},{9,1},{17,25},{25,17},{2,10},{10... | collective-permute-start | bytes 3145736 | tf_op jit(solution)/shard_map/ppermute | solution.py:17
  224.8 39.3 %collective-permute-start.18 = (bf16[1024,512]{1,0:T(8,128)(2,1)}, bf16[1024,512]{1,0:T(8,128)(2,1)}, u32[]{:S(2)}, u32[]{:S(2)}) collective-permute-start(bf16[1024,512]{1,0:T(8,128)(2,1)} %get-tuple-element.36), channel_id=1, source_target_pairs={{0,16},{8,24},{16,0},{24,8},{1,17},{9,25},{17,1},{25,9},{2,18},{10... | collective-permute-start | bytes 3145736 | tf_op jit(solution)/shard_map/ppermute | solution.py:17
  225.4 1.0 copy-start.1
  225.4 38.7 %collective-permute-start.17 = (bf16[1024,512]{1,0:T(8,128)(2,1)}, bf16[1024,512]{1,0:T(8,128)(2,1)}, u32[]{:S(2)}, u32[]{:S(2)}) collective-permute-start(bf16[1024,512]{1,0:T(8,128)(2,1)} %get-tuple-element.35), channel_id=1, source_target_pairs={{0,8},{8,0},{16,24},{24,16},{1,9},{9,1},{17,25},{25,17},{2,10},{10... | collective-permute-start | bytes 3145736 | tf_op jit(solution)/shard_map/ppermute | solution.py:17
  249.2 31.9 %collective-permute-start.12 = (bf16[1024,512]{1,0:T(8,128)(2,1)}, bf16[1024,512]{1,0:T(8,128)(2,1)S(1)}, u32[]{:S(2)}, u32[]{:S(2)}) collective-permute-start(bf16[1024,512]{1,0:T(8,128)(2,1)} %copy-done.1), channel_id=1, source_target_pairs={{0,8},{8,0},{16,24},{24,16},{1,9},{9,1},{17,25},{25,17},{2,10},{10... | collective-permute-start | bytes 3145736 | tf_op jit(solution)/shard_map/ppermute | solution.py:17
  250.4 31.7 %collective-permute-start.11 = (bf16[1024,512]{1,0:T(8,128)(2,1)}, bf16[1024,512]{1,0:T(8,128)(2,1)}, u32[]{:S(2)}, u32[]{:S(2)}) collective-permute-start(bf16[1024,512]{1,0:T(8,128)(2,1)} %collective-permute-done.9.refs_9_), channel_id=1, source_target_pairs={{0,16},{8,24},{16,0},{24,8},{1,17},{9,25},{17,1},{25,9},{2,18},{10... | collective-permute-start | bytes 3145736 | tf_op jit(solution)/shard_map/ppermute | solution.py:17
  281.2 1.0 copy-start.2
